TPU v7x, 512 devices: a whole 4x8x8 slice. The times are simulated.
512 devices in a mesh: prompt: 16 (over x, z_hi), sample: 32 (over y, z_lo, core).
Axes of the slice: x: 4, y: 8, z: 8 (z_hi: 4, z_lo: 2; z = z_hi * 2 + z_lo), core: 2. Of those that a mesh axis runs over, the one named last changes fastest.
Arguments:
- prompt_query: bfloat16 [2048, 4096], P('sample', 'prompt'), may hold values from -120 to 120
- prompt_grad: bfloat16 [2048, 4096], P('sample', 'prompt'), may hold values from -24 to 24
- prompt_out: bfloat16 [2048, 4096], P('sample', 'prompt'), may hold values from -1.75 to 1.75
- prompt_key_codes: bfloat16 [2048, 512], P('prompt'), may hold values from -5 to 5
- prompt_value_codes: bfloat16 [2048, 512], P('prompt'), may hold values from -5 to 5
- key_scales: float32 [64, 4], P('prompt'), may hold values from 0.5 to 2
- value_scales: float32 [64, 4], P('prompt'), may hold values from 0.5 to 2
- response_query: bfloat16 [32, 256, 4096], P('sample', None, 'prompt'), may hold values from -120 to 120
- response_grad: bfloat16 [32, 256, 4096], P('sample', None, 'prompt'), may hold values from -24 to 24
- response_out: bfloat16 [32, 256, 4096], P('sample', None, 'prompt'), may hold values from -1.75 to 1.75
- response_key: bfloat16 [32, 256, 512], P('sample', 'prompt'), may hold values from -6 to 6
- response_value: bfloat16 [32, 256, 512], P('sample', 'prompt'), may hold values from -6 to 6
- lengths: int32 [32], P('sample'), may hold values from 128 to 256, as said below
Outputs:
- prompt_dq: bfloat16 [2048, 4096], P('sample', 'prompt')
- prompt_dk: bfloat16 [2048, 512], P(('prompt', 'sample'))
- prompt_dv: bfloat16 [2048, 512], P(('prompt', 'sample'))
- response_dq: bfloat16 [32, 256, 4096], P('sample', None, 'prompt')
- response_dk: bfloat16 [32, 256, 512], P('sample', 'prompt')
- response_dv: bfloat16 [32, 256, 512], P('sample', 'prompt')
Inputs may be any that keep to these rules, and one draw needn't show every extreme that they name: `lengths`: each length is a multiple of 128; some response has length 256.
All inputs are finite; a program needn't handle non-finite values.
Results may differ from a plain program's by a relative error of at most 0.035.
Values may be sent and summed in bfloat16 or wider, within the bound.
A program may use at most 64 MiB of HBM per device.

v0:
```python
import math

import jax
import jax.numpy as jnp
from jax import lax
from jax.sharding import PartitionSpec as P

QH = 32
KVH = 4
HD = 128
SBLK = 32


NEG_FILL = -1e30


def dequantize(codes, scales):
    row_total = codes.shape[0]
    blocks = codes.astype(jnp.float32).reshape(row_total // SBLK, SBLK, KVH, HD)
    blocks = blocks * scales[:, None, :, None]
    return blocks.astype(jnp.bfloat16).reshape(row_total, KVH, HD)


def softmax_rows(scores, visible):
    masked = jnp.where(visible, scores, NEG_FILL)
    highest = jnp.max(masked, axis=-1, keepdims=True)
    powers = jnp.where(visible, jnp.exp(masked - highest), 0.0)
    return powers / jnp.sum(powers, axis=-1, keepdims=True)


def spread_heads(paired, repeats):
    swapped = jnp.swapaxes(paired, 0, 1)
    wide = jnp.broadcast_to(swapped[:, None], (swapped.shape[0], repeats) + swapped.shape[1:])
    return wide.reshape((swapped.shape[0] * repeats,) + swapped.shape[1:])


def join_heads(received, repeats):
    row_count = received.shape[1]
    summed = received.reshape(KVH, repeats, row_count, 2, HD).sum(axis=1)
    return jnp.transpose(summed, (1, 2, 0, 3)).reshape(row_count, 2, KVH * HD)


def shards(
    prompt_query,
    prompt_grad,
    prompt_out,
    prompt_key_codes,
    prompt_value_codes,
    key_scales,
    value_scales,
    response_query,
    response_grad,
    response_out,
    response_key,
    response_value,
    lengths,
):
    inv_root = 1.0 / math.sqrt(HD)
    group_size = QH // KVH
    prompt_count = lax.axis_size("prompt")
    prompt_place = lax.axis_index("prompt")
    sample_place = lax.axis_index("sample")
    query_rows = prompt_query.shape[0]
    heads_here = prompt_query.shape[1] // HD
    block_rows = prompt_key_codes.shape[0]
    prompt_total = block_rows * prompt_count
    resp_total = response_query.shape[1]
    resp_block = response_key.shape[1]
    repeats = group_size // heads_here
    own_head = prompt_place * heads_here // group_size
    paired = jnp.concatenate(
        [dequantize(prompt_key_codes, key_scales), dequantize(prompt_value_codes, value_scales)],
        axis=2,
    )
    outgoing = spread_heads(paired, repeats)
    resp_paired = jnp.concatenate(
        [
            response_key[0].reshape(resp_block, KVH, HD),
            response_value[0].reshape(resp_block, KVH, HD),
        ],
        axis=2,
    )
    incoming = lax.all_to_all(outgoing, "prompt", split_axis=0, concat_axis=0, tiled=True)
    resp_every = lax.all_gather(resp_paired, "prompt", axis=0, tiled=True)
    resp_table = lax.dynamic_index_in_dim(resp_every, own_head, 1, False)
    prompt_table = incoming.reshape(prompt_total, 2 * HD)
    key_table = jnp.concatenate([prompt_table[:, :HD], resp_table[:, :HD]], axis=0)
    value_table = jnp.concatenate([prompt_table[:, HD:], resp_table[:, HD:]], axis=0)
    resp_steps = jnp.arange(resp_total, dtype=jnp.int32)
    row_place = jnp.concatenate(
        [sample_place * query_rows + jnp.arange(query_rows, dtype=jnp.int32), resp_steps]
    )
    key_place = jnp.concatenate([jnp.arange(prompt_total, dtype=jnp.int32), resp_steps])
    resp_row = jnp.arange(query_rows + resp_total, dtype=jnp.int32) >= query_rows
    resp_key = jnp.arange(prompt_total + resp_total, dtype=jnp.int32) >= prompt_total
    earlier = key_place[None, :] <= row_place[:, None]
    length = lengths[0]
    visible = jnp.where(
        resp_row[:, None],
        jnp.logical_or(jnp.logical_not(resp_key)[None, :], earlier & (key_place[None, :] < length)),
        earlier & jnp.logical_not(resp_key)[None, :],
    )
    live_rows = resp_steps < length
    resp_grad = jnp.where(live_rows[:, None], response_grad[0], jnp.zeros_like(response_grad[0]))
    all_query = jnp.concatenate([prompt_query, response_query[0]], axis=0).reshape(
        -1, heads_here, HD
    )
    all_grad = jnp.concatenate([prompt_grad, resp_grad], axis=0).reshape(-1, heads_here, HD)
    all_out = jnp.concatenate([prompt_out, response_out[0]], axis=0).reshape(-1, heads_here, HD)
    all_delta = jnp.sum(all_grad.astype(jnp.float32) * all_out.astype(jnp.float32), axis=-1)

    def one_head(sums_carry, head_items):
        one_query, one_grad, one_delta = head_items
        scores = (
            jnp.einsum("qd,kd->qk", one_query, key_table, preferred_element_type=jnp.float32)
            * inv_root
        )
        attention = softmax_rows(scores, visible)
        weights = attention.astype(jnp.bfloat16)
        grad_prob = jnp.einsum(
            "qd,kd->qk", one_grad, value_table, preferred_element_type=jnp.float32
        )
        grad_score = (attention * (grad_prob - one_delta[:, None])).astype(jnp.bfloat16)
        grad_query = jnp.dot(grad_score, key_table, preferred_element_type=jnp.float32) * inv_root
        grad_key = (
            jnp.einsum("qk,qd->kd", grad_score, one_query, preferred_element_type=jnp.float32)
            * inv_root
        )
        grad_value = jnp.einsum("qk,qd->kd", weights, one_grad, preferred_element_type=jnp.float32)
        return ((sums_carry[0] + grad_key, sums_carry[1] + grad_value), grad_query)

    zero_sums = jnp.zeros((prompt_total + resp_total, HD), jnp.float32)
    head_items = (
        jnp.swapaxes(all_query, 0, 1),
        jnp.swapaxes(all_grad, 0, 1),
        jnp.swapaxes(all_delta, 0, 1),
    )
    (key_sums, value_sums), query_grads = lax.scan(one_head, (zero_sums, zero_sums), head_items)
    query_grads = jnp.swapaxes(query_grads, 0, 1).astype(jnp.bfloat16)
    prompt_dq = query_grads[:query_rows].reshape(query_rows, heads_here * HD)
    response_dq = query_grads[query_rows:].reshape(1, resp_total, heads_here * HD)
    terms = jnp.concatenate([key_sums, value_sums], axis=1)
    prompt_terms = terms[:prompt_total]
    resp_terms = terms[prompt_total:].reshape(prompt_count, resp_block, 2 * HD)
    back_prompt, back_resp = (
        lax.all_to_all(
            prompt_terms.reshape(prompt_count, block_rows, 2 * HD),
            "prompt",
            split_axis=0,
            concat_axis=0,
            tiled=True,
        ),
        lax.all_to_all(resp_terms, "prompt", split_axis=0, concat_axis=0, tiled=True),
    )
    arranged = join_heads(back_prompt, repeats)
    own_rows = lax.psum_scatter(
        arranged.astype(jnp.bfloat16), "sample", scatter_dimension=0, tiled=True
    ).astype(jnp.float32)
    resp_rows = join_heads(back_resp, repeats)
    prompt_dk = own_rows[:, 0].astype(jnp.bfloat16)
    prompt_dv = own_rows[:, 1].astype(jnp.bfloat16)
    response_dk = resp_rows[:, 0].astype(jnp.bfloat16).reshape(1, resp_block, KVH * HD)
    response_dv = resp_rows[:, 1].astype(jnp.bfloat16).reshape(1, resp_block, KVH * HD)
    return (prompt_dq, prompt_dk, prompt_dv, response_dq, response_dk, response_dv)


def solution(mesh):
    placed = (
        P("sample", "prompt"),
        P("sample", "prompt"),
        P("sample", "prompt"),
        P("prompt", None),
        P("prompt", None),
        P("prompt", None),
        P("prompt", None),
        P("sample", None, "prompt"),
        P("sample", None, "prompt"),
        P("sample", None, "prompt"),
        P("sample", "prompt", None),
        P("sample", "prompt", None),
        P("sample"),
    )
    return jax.shard_map(
        shards,
        mesh=mesh,
        in_specs=placed,
        out_specs=(
            P("sample", "prompt"),
            P(("prompt", "sample"), None),
            P(("prompt", "sample"), None),
            P("sample", None, "prompt"),
            P("sample", "prompt", None),
            P("sample", "prompt", None),
        ),
        check_vma=False,
    )
```

profile of v0, /device:TPU:1, one launch (start us, length us, event | category | flops | bytes accessed | tf_op | source)
XLA Modules:
  0.0 420.7 jit_solution(9029390378764063900)
XLA Ops:
  7.2 1.0 reshape.145
  8.2 1.0 reshape.143
  9.2 0.7 mul.51
  9.8 0.2 multiply_convert_fusion
  10.0 0.7 mul.47
  10.7 0.2 multiply_convert_fusion.1
  11.0 0.1 maximum_bitcast_fusion
  11.2 1.1 broadcast_in_dim.56
  12.3 13.6 %all-to-all-start = ((bf16[16,128,256]{2,1,0:T(8,128)(2,1)}), bf16[16,128,256]{2,1,0:T(8,128)(2,1)S(1)}, u32[]{:S(2)}, u32[]{:S(2)}) async-start(bf16[16,128,256]{2,1,0:T(8,128)(2,1)} %bitcast.6), calls=%async_computation | async-start | bytes 2097152 | tf_op jit(solution)/shard_map/all_to_all | solution.py:83
  26.7 0.1 bitcast_select_fusion
  26.9 0.1 copy.52
  27.0 0.1 copy.53
  27.1 0.4 multiply_reduce_fusion
  27.5 0.7 copy.56
  28.2 0.7 copy.55
  28.9 0.1 copy.47
  29.0 0.1 copy.62
  29.1 0.1 maximum_bitcast_fusion.1
  29.3 0.8 copy.54
  30.1 0.6 iota_compare_fusion.1
  30.6 0.7 pad_add_fusion.1
  31.3 0.6 fusion.27
  31.9 48.2 %all_gather.3 = bf16[256,4,256]{2,0,1:T(8,128)(2,1)S(1)} all-gather(bf16[16,4,256]{2,0,1:T(8,128)(2,1)S(1)} %pad_maximum_fusion.3), channel_id=1, replica_groups=mesh['prompt'=16,'sample'=32] {'prompt'}, dimensions={0}, use_global_device_ids=true | all-gather | bytes 557056 | tf_op jit(solution)/shard_map/all_gather | solution.py:84
  80.2 0.9 pad_maximum_fusion
  81.1 28.6 %while.15 = (s32[]{:T(128)}, f32[2304,128]{1,0:T(8,128)}, f32[2304,128]{1,0:T(8,128)}, bf16[2,320,128]{2,1,0:T(8,128)(2,1)}, bf16[2,320,128]{2,1,0:T(8,128)(2,1)...) while((s32[]{:T(128)}, f32[2304,128]{1,0:T(8,128)}, ...), condition=%wide.region_4.5_spmd.clone, body=%wide.region_1.4_spmd.clone.sunk | while | flops 971775360 | bytes 28326292 | solution.py:138
  81.1 2.2 fusion.59
  83.3 0.6 copy-done.16
  83.9 1.9 fusion.60
  85.9 3.7 convolution_add_fusion.2
  89.7 1.9 fusion.61
  91.6 1.8 fusion.62
  93.3 0.6 fusion.63
  93.9 0.6 copy-done.6
  94.6 2.2 fusion.59
  96.8 0.6 copy-done.16
  97.4 1.9 fusion.60
  99.3 4.1 convolution_add_fusion.2
  103.5 1.8 fusion.61
  105.4 3.1 fusion.62
  108.5 0.6 fusion.63
  109.1 0.6 copy-done.6
  109.7 1.5 constant_dynamic-update-slice_fusion.1
  111.2 0.2 copy-done.3
  111.5 1.4 copy-done.1
  112.9 1.5 slice.57
  114.4 4.3 %all-to-all-start.1 = ((f32[16,128,256]{2,1,0:T(8,128)}), f32[16,128,256]{2,1,0:T(8,128)S(1)}, u32[]{:S(2)}, u32[]{:S(2)}) async-start(f32[16,128,256]{2,1,0:T(8,128)} %bitcast.89), calls=%async_computation.1 | async-start | bytes 4194304 | tf_op jit(solution)/shard_map/all_to_all | solution.py:146
  118.6 1.7 slice.59
  120.3 34.6 %all-to-all-done.1 = f32[16,128,256]{2,1,0:T(8,128)S(1)} async-done(((f32[16,128,256]{2,1,0:T(8,128)}), f32[16,128,256]{2,1,0:T(8,128)S(1)}, u32[]{:S(2)}, u32[]{:S(2)}) %all-to-all-start.1) | async-done | bytes 2097184 | tf_op jit(solution)/shard_map/all_to_all | solution.py:146
  155.0 17.4 %all-to-all-start.2 = ((f32[16,16,256]{2,1,0:T(8,128)}), f32[16,16,256]{2,1,0:T(8,128)S(1)}, u32[]{:S(2)}, u32[]{:S(2)}) async-start(f32[16,16,256]{2,1,0:T(8,128)} %bitcast.20), calls=%async_computation.2 | async-start | bytes 524288 | tf_op jit(solution)/shard_map/all_to_all | solution.py:153
  172.4 0.2 all-reduce.3.cloned.1.call-start
  172.6 1.3 dynamic-slice
  174.6 2.3 reshape.137
  176.9 1.3 reduce_sum.37
  178.2 0.2 copy.58
  178.4 0.8 copy.59
  179.3 0.6 copy_bitcast_fusion
  179.9 0.1 copy.60
  180.1 0.7 reshape.138
  180.8 2.1 all-to-all-done.2
  182.9 0.1 reshape.140
  183.0 0.1 reduce_sum.38
  183.2 0.6 slice_bitcast_fusion.1
  183.8 228.8 %all-reduce.3.cloned.1.call-done = bf16[128,2,512]{2,0,1:T(8,128)(2,1)} async-done(((bf16[128,2,512]{2,0,1:T(8,128)(2,1)}), bf16[128,2,512]{2,0,1:T(8,128)(2,1)}) %all-reduce.3.cloned.1.call-update) | async-done | bytes 262160
  412.6 1.3 dynamic-slice_bitcast_fusion.1
  (107 shorter events, 0.6 us)
Async XLA Ops:
  10.9 15.0 %copy-start.23 = (bf16[1,16,512]{2,1,0:T(8,128)(2,1)S(1)}, bf16[1,16,512]{2,1,0:T(8,128)(2,1)}, u32[]{:S(2)}) copy-start(bf16[1,16,512]{2,1,0:T(8,128)(2,1)} %param.25) | copy-start | bytes 49156
  11.0 15.0 %copy-start.24 = (bf16[1,16,512]{2,1,0:T(8,128)(2,1)S(1)}, bf16[1,16,512]{2,1,0:T(8,128)(2,1)}, u32[]{:S(2)}) copy-start(bf16[1,16,512]{2,1,0:T(8,128)(2,1)} %param.26) | copy-start | bytes 49156
  11.0 15.7 %copy-start.9 = (bf16[1,256,256]{2,1,0:T(8,128)(2,1)S(1)}, bf16[1,256,256]{2,1,0:T(8,128)(2,1)}, u32[]{:S(2)}) copy-start(bf16[1,256,256]{2,1,0:T(8,128)(2,1)} %param.23) | copy-start | bytes 393220
  11.0 15.8 %copy-start.20 = (bf16[64,256]{1,0:T(8,128)(2,1)S(1)}, bf16[64,256]{1,0:T(8,128)(2,1)}, u32[]{:S(2)}) copy-start(bf16[64,256]{1,0:T(8,128)(2,1)} %param.16) | copy-start | bytes 98308
  11.2 15.7 %copy-start.10 = (bf16[1,256,256]{2,1,0:T(8,128)(2,1)S(1)}, bf16[1,256,256]{2,1,0:T(8,128)(2,1)}, u32[]{:S(2)}) copy-start(bf16[1,256,256]{2,1,0:T(8,128)(2,1)} %param.24) | copy-start | bytes 393220
  11.2 15.9 %copy-start.22 = (bf16[64,256]{1,0:T(8,128)(2,1)S(1)}, bf16[64,256]{1,0:T(8,128)(2,1)}, u32[]{:S(2)}) copy-start(bf16[64,256]{1,0:T(8,128)(2,1)} %param.17) | copy-start | bytes 98308
  12.3 16.6 %copy-start.11 = (bf16[1,256,256]{2,1,0:T(8,128)(2,1)S(1)}, bf16[1,256,256]{2,1,0:T(8,128)(2,1)}, u32[]{:S(2)}) copy-start(bf16[1,256,256]{2,1,0:T(8,128)(2,1)} %param.22) | copy-start | bytes 393220
  12.3 16.7 %copy-start.21 = (bf16[64,256]{1,0:T(8,128)(2,1)S(1)}, bf16[64,256]{1,0:T(8,128)(2,1)}, u32[]{:S(2)}) copy-start(bf16[64,256]{1,0:T(8,128)(2,1)} %param.15) | copy-start | bytes 98308
  12.3 67.8 %all-to-all-start = ((bf16[16,128,256]{2,1,0:T(8,128)(2,1)}), bf16[16,128,256]{2,1,0:T(8,128)(2,1)S(1)}, u32[]{:S(2)}, u32[]{:S(2)}) async-start(bf16[16,128,256]{2,1,0:T(8,128)(2,1)} %bitcast.6), calls=%async_computation | async-start | bytes 2097152 | tf_op jit(solution)/shard_map/all_to_all | solution.py:83
  81.1 2.8 copy-start.12
  81.1 2.8 copy-start.14
  81.1 2.8 copy-start.25
  83.3 0.6 copy-start.16
  85.8 3.8 copy-start.19
  85.8 3.8 copy-start.4
  85.8 3.8 copy-start.8
  85.8 3.8 copy-start.13
  85.8 3.8 copy-start.15
  85.8 3.8 copy-start.17
  85.9 3.8 copy-start.18
  85.9 3.8 copy-start.26
  89.7 1.9 copy-start.2
  91.5 1.8 copy-start.5
  93.9 0.7 copy-start.6
  94.6 2.8 copy-start.12
  94.6 2.8 copy-start.14
  94.6 2.8 copy-start.25
  96.8 0.6 copy-start.16
  99.3 4.2 copy-start.19
  99.3 4.2 copy-start.4
  99.3 4.2 copy-start.8
  99.3 4.2 %copy-start.13 = (pred[2304]{0:T(1024)(128)(4,1)S(1)}, pred[2304]{0:T(1024)(128)(4,1)}, u32[]{:S(2)}) copy-start(pred[2304]{0:T(1024)(128)(4,1)} %get-tuple-element.329) | copy-start | bytes 6916 | tf_op jit(solution)/shard_map/while
  99.3 4.2 %copy-start.15 = (s32[320]{0:T(512)S(1)}, s32[320]{0:T(512)}, u32[]{:S(2)}) copy-start(s32[320]{0:T(512)} %get-tuple-element.330) | copy-start | bytes 3844 | tf_op jit(solution)/shard_map/while
  99.3 4.2 %copy-start.17 = (f32[320]{0:T(512)S(1)}, f32[320]{0:T(512)}, u32[]{:S(2)}) copy-start(f32[320]{0:T(512)} %copy-done.16) | copy-start | bytes 3844 | tf_op jit(solution)/shard_map/while
  99.3 4.2 %copy-start.18 = (f32[320]{0:T(512)S(1)}, f32[320]{0:T(512)}, u32[]{:S(2)}) copy-start(f32[320]{0:T(512)} %fusion.60) | copy-start | bytes 3844 | tf_op jit(solution)/shard_map/while
  99.3 4.2 %copy-start.26 = (pred[320]{0:T(512)(128)(4,1)S(1)}, pred[320]{0:T(512)(128)(4,1)}, u32[]{:S(2)}) copy-start(pred[320]{0:T(512)(128)(4,1)} %get-tuple-element.333) | copy-start | bytes 964 | tf_op jit(solution)/shard_map/while
  103.5 1.9 copy-start.2
  105.4 3.1 copy-start.5
  109.1 0.7 copy-start.6
  109.7 1.6 copy-start.3
  111.5 1.4 copy-start.1
  114.4 40.6 %all-to-all-start.1 = ((f32[16,128,256]{2,1,0:T(8,128)}), f32[16,128,256]{2,1,0:T(8,128)S(1)}, u32[]{:S(2)}, u32[]{:S(2)}) async-start(f32[16,128,256]{2,1,0:T(8,128)} %bitcast.89), calls=%async_computation.1 | async-start | bytes 4194304 | tf_op jit(solution)/shard_map/all_to_all | solution.py:146
  155.0 18.9 %copy-start = (f32[16,128,256]{2,1,0:T(8,128)}, f32[16,128,256]{2,1,0:T(8,128)S(1)}, u32[]{:S(2)}) copy-start(f32[16,128,256]{2,1,0:T(8,128)S(1)} %all-to-all-done.1) | copy-start | bytes 6291460
  155.0 27.9 %all-to-all-start.2 = ((f32[16,16,256]{2,1,0:T(8,128)}), f32[16,16,256]{2,1,0:T(8,128)S(1)}, u32[]{:S(2)}, u32[]{:S(2)}) async-start(f32[16,16,256]{2,1,0:T(8,128)} %bitcast.20), calls=%async_computation.2 | async-start | bytes 524288 | tf_op jit(solution)/shard_map/all_to_all | solution.py:153
  172.4 240.2 %all-reduce.3.cloned.1.call-start = ((), (), s32[]{:S(2)}) async-start(), calls=%async_computation.3 | async-start | bytes 524288
  176.9 2.4 copy-start.7
Sparse Core Ops, SparseCore 0:
  179.4 233.1 all-reduce.2
where the time goes:
time: 421 us
  waiting for transfers between devices  265 us (63%)
  blocking collectives  48.2 us (11%)
  starting transfers between devices  35.5 us (8%)
  local copies, waits for them, and re-layouts  24.4 us (6%)
  matrix products  21.9 us (5%)
  between operations  15.8 us (4%)
  other arithmetic  9.16 us (2%)
    unnamed x2, waiting for transfers between devices  229 us
    all_gather x1, blocking collectives, shards(): resp_every = lax.all_gather(resp_paired, 'prompt', axis=0, tiled=True)  48.2 us
    all_to_all x1, waiting for transfers between devices, shards(): lax.all_to_all(prompt_terms.reshape(prompt_count, block_rows, 2 * HD), 'p...  34.6 us
    all_to_all x1, starting transfers between devices, shards(): lax.all_to_all(resp_terms, 'prompt', split_axis=0, concat_axis=0, tiled=T...  17.4 us
    all_to_all x1, starting transfers between devices, shards(): lax.all_to_all(outgoing, 'prompt', split_axis=0, concat_axis=0, tiled=True)  13.6 us
  transfers between devices with their start and end apart: 4, of which 3 were waited for; matrix products, arithmetic and copies ran while one was open for 4% of the time, Pallas kernels for 0%

commit v1 on v0

v1 whole, which is shorter than its diff:
```python
import math

import jax
import jax.numpy as jnp
from jax import lax
from jax.experimental import pallas as pl
from jax.experimental.pallas import tpu as pltpu
from jax.sharding import PartitionSpec as P

HD = 128
SBLK = 32
MESH = pl.DeviceIdType.MESH
NEG = -1e30
F32 = jnp.float32
BF = jnp.bfloat16
LOG2E = 1.4426950408889634

NX, NY, NZ, NZH = 4, 8, 8, 4
RESP = 256
PROWS = 64
RL = 2 * RESP
LANES = RL + 2 * PROWS
GROUP = 512


def dot_t(a, b):
    return lax.dot_general(a, b, (((1,), (1,)), ((), ())), preferred_element_type=F32)


def dot_n(a, b):
    return lax.dot_general(a, b, (((1,), (0,)), ((), ())), preferred_element_type=F32)


def dot_l(a, b):
    return lax.dot_general(a, b, (((0,), (0,)), ((), ())), preferred_element_type=F32)


def kernel(
    pq, pg, po, kc, vc, ks, vs, rq, rg, ro, rk, rv, ln,
    o_dq, o_dk, o_dv, o_rdq, o_rdk, o_rdv,
    qm, gm, om, codes, deq, table, rsend, rtab, kr, vr, S, Sr, dqs, dqt,
    gout, r1, ady, adz, ray, raz, bdy, bdz, rby, rbz, fin, rfin, rgs, rgr,
    in_sem, rin_sem, out_sem,
    p_ss, p_rs, q_ss, q_rs, d_ss, d_rs, e_ss, e_rs, ya_ss, ya_rs, za_ss, za_rs,
    yb_ss, yb_rs, zb_ss, zb_rs, f_ss, f_rs, g_ss, g_rs,
):
    p = lax.axis_index("prompt")
    s = lax.axis_index("sample")
    x, zh = p // 4, p % 4
    y, zl, c = s // 4, (s // 2) % 2, s % 2
    z = zh * 2 + zl
    sg = 2 * zl - 1
    inv = 1.0 / math.sqrt(HD)

    def dev(xx, yy, zz, cc):
        return (xx * 4 + zz // 2, yy * 4 + (zz % 2) * 2 + cc)

    def wrap(v, n):
        return lax.rem(v + 2 * n, n)

    def remote(src, dst, ss, rs, to):
        return pltpu.make_async_remote_copy(src, dst, ss, rs, device_id=to, device_id_type=MESH)

    sib = dev(x, y, z, 1 - c)

    bar = pltpu.get_barrier_semaphore()
    partners = []
    for dx in range(NX):
        for dz in range(NZ):
            if dx or dz:
                partners.append(dev(wrap(x + dx, NX), y, wrap(z + dz, NZ), c))
    for dy in range(1, NY):
        partners.append(dev(x, wrap(y + dy, NY), z, c))
    for dx in range(NX):
        for zz in range(2):
            partners.append(dev(wrap(x + dx, NX), y, zh * 2 + zz, 1 - c))
    for to in partners:
        pl.semaphore_signal(bar, inc=1, device_id=to, device_id_type=MESH)

    @pl.when(c == 0)
    def _():
        pltpu.make_async_copy(kc, codes, in_sem.at[12]).start()

    @pl.when(c == 1)
    def _():
        pltpu.make_async_copy(vc, codes, in_sem.at[12]).start()

    rloads = []
    for g in range(NX):
        for i, ref in enumerate((rk, rv)):
            rloads.append(
                pltpu.make_async_copy(
                    ref.at[0, :, pl.ds(g * HD, HD)], rsend.at[g, pl.ds(16 * i, 16)], rin_sem.at[g * 2 + i]
                )
            )
    for cp in rloads:
        cp.start()
    loads = []
    for i, (pref, rref, dst) in enumerate(((pq, rq, qm), (pg, rg, gm), (po, ro, om))):
        for h in range(2):
            loads.append(
                pltpu.make_async_copy(
                    rref.at[0, :, pl.ds(h * HD, HD)], dst.at[pl.ds(h * RESP, RESP)], in_sem.at[i * 4 + h]
                )
            )
            loads.append(
                pltpu.make_async_copy(
                    pref.at[:, pl.ds(h * HD, HD)], dst.at[pl.ds(RL + h * PROWS, PROWS)], in_sem.at[i * 4 + 2 + h]
                )
            )
    for cp in loads:
        cp.start()

    pltpu.make_async_copy(kc, codes, in_sem.at[12]).wait()
    for g in range(NX):
        for b in range(128 // SBLK):
            scale = jnp.where(c == 0, ks[b, g], vs[b, g])
            block = codes[b * SBLK : (b + 1) * SBLK, g * HD : (g + 1) * HD].astype(F32) * scale
            deq[g, b * SBLK : (b + 1) * SBLK, :] = block.astype(BF)
    own_rows = pl.ds(pl.multiple_of(x * 128, 128), 128)
    table[c, zh, own_rows, :] = deq[x]
    for cp in rloads:
        cp.wait()

    pl.semaphore_wait(bar, len(partners))

    psends = []
    for d in (1, 2, 3):
        for dx in range(NX):
            psends.append((wrap(x + dx, NX), wrap(z + sg * d, NZ)))
    for dx in (1, 2, 3):
        psends.append((wrap(x + dx, NX), z))
    pcopies = []
    for i, (xt, zt) in enumerate(psends):
        cp = remote(deq.at[xt], table.at[c, zh, own_rows], p_ss.at[i], p_rs.at[p], dev(xt, y, zt, c))
        cp.start()
        pcopies.append(cp)
    qcopies = []
    for k in range(1, 16):
        pt = wrap(p + k, 16)
        cp = remote(rsend.at[pt // 4], rtab.at[p], q_ss.at[k], q_rs.at[p], (pt, s))
        cp.start()
        qcopies.append(cp)
    rtab[p] = rsend[x]

    groups = [zh, wrap(zh + sg, NZH), wrap(zh - sg, NZH), wrap(zh + 2, NZH)]

    dcopies = []
    for k in range(4):
        zg = groups[k]
        for dx in range(NX):
            xs = wrap(x + dx, NX)
            rows = pl.ds(pl.multiple_of(xs * 128, 128), 128)
            piece = table.at[c, zg, rows]
            if k or dx:
                remote(piece, piece, p_ss.at[0], p_rs.at[xs * 4 + zg], sib).wait_recv()
        cp = remote(table.at[c, zg], table.at[c, zg], d_ss.at[k], d_rs.at[zg], sib)
        cp.start()
        dcopies.append(cp)

    for cp in loads:
        cp.wait()
    length = ln[0]
    live = lax.broadcasted_iota(jnp.int32, (RESP, HD), 0) < length
    for h in range(2):
        block = gm[h * RESP : (h + 1) * RESP, :]
        gm[h * RESP : (h + 1) * RESP, :] = jnp.where(live, block, jnp.zeros_like(block))
    delta = jnp.sum((gm[...].astype(F32) * om[...].astype(F32)).T, axis=0, keepdims=True)

    for k in range(1, 16):
        ps = wrap(p + k, 16)
        remote(rtab.at[ps], rtab.at[ps], q_ss.at[0], q_rs.at[ps], sib).wait_recv()
    for i in range(16):
        kr[i * 16 : (i + 1) * 16, :] = rtab[i, 0:16, :]
        vr[i * 16 : (i + 1) * 16, :] = rtab[i, 16:32, :]

    for k in range(4):
        zg = groups[k]
        other = table.at[1 - c, zg]
        remote(other, other, d_ss.at[0], d_rs.at[zg], sib).wait_recv()

    u = lax.broadcasted_iota(jnp.int32, (RESP, RESP), 0)
    t = lax.broadcasted_iota(jnp.int32, (RESP, RESP), 1)
    near = (u <= t) & (u < length)
    sr = dot_t(kr[...], qm[0:RL, :])
    tops = []
    for h in range(2):
        part = jnp.where(near, sr[:, h * RESP : (h + 1) * RESP], NEG)
        Sr[:, h * RESP : (h + 1) * RESP] = part
        tops.append(jnp.max(part, axis=0, keepdims=True))
    top = jnp.concatenate(tops + [jnp.full((1, 2 * PROWS), NEG, F32)], axis=1)

    def group_of(k):
        step = jnp.where(k == 1, sg, jnp.where(k == 2, -sg, jnp.where(k == 3, 2, 0)))
        return lax.rem(zh + step + 4, 4)

    def scores(k, top):
        zg = group_of(k)
        keys = table[0, zg]
        far = dot_t(keys, qm[0:RL, :])
        S[zg, :, 0:RL] = far
        row = lax.broadcasted_iota(jnp.int32, (GROUP, 2 * PROWS), 0)
        lane = lax.broadcasted_iota(jnp.int32, (GROUP, 2 * PROWS), 1)
        place = (row // 128) * 512 + zg * 128 + row % 128
        own = dot_t(keys, qm[RL:LANES, :])
        own = jnp.where(place <= s * PROWS + lane % PROWS, own, NEG)
        S[zg, :, RL:LANES] = own
        best = jnp.concatenate([jnp.max(far, axis=0, keepdims=True), jnp.max(own, axis=0, keepdims=True)], axis=1)
        return jnp.maximum(top, best)

    top = lax.fori_loop(0, 4, scores, top)

    er = jnp.exp2((Sr[...] - top[:, 0:RL]) * (inv * LOG2E))
    Sr[...] = er
    total = jnp.concatenate([jnp.sum(er, axis=0, keepdims=True), jnp.zeros((1, 2 * PROWS), F32)], axis=1)

    def powers(k, total):
        zg = group_of(k)
        e = jnp.exp2((S[zg] - top) * (inv * LOG2E))
        S[zg] = e
        return total + jnp.sum(e, axis=0, keepdims=True)

    total = lax.fori_loop(0, 4, powers, total)
    rtotal = 1.0 / total

    prob = Sr[...] * rtotal[:, 0:RL]
    dp = dot_t(vr[...], gm[0:RL, :])
    ds = (prob * (dp - delta[:, 0:RL])).astype(BF)
    dqt[:, 0:RL] = dot_l(kr[...], ds)
    dqt[:, RL:LANES] = jnp.zeros((HD, 2 * PROWS), F32)
    dkr = (dot_n(ds, qm[0:RL, :]) * inv).astype(BF)
    dvr = dot_n(prob.astype(BF), gm[0:RL, :]).astype(BF)
    for i in range(16):
        rgs[i, 0:16, :] = dkr[i * 16 : (i + 1) * 16, :]
        rgs[i, 16:32, :] = dvr[i * 16 : (i + 1) * 16, :]
    gcopies = []
    for k in range(1, 16):
        pt = wrap(p + k, 16)
        cp = remote(rgs.at[pt], rgr.at[p], g_ss.at[k], g_rs.at[p], (pt, s))
        cp.start()
        gcopies.append(cp)
    rgr[p] = rgs[p]

    def grads(k, _):
        zg = group_of(k)
        prob = S[zg] * rtotal
        dp = dot_t(table[1, zg], gm[...])
        ds = (prob * (dp - delta)).astype(BF)
        dqt[...] += dot_l(table[0, zg], ds)
        gout[0, zg] = (dot_n(ds, qm[...]) * inv).astype(BF)
        gout[1, zg] = dot_n(prob.astype(BF), gm[...]).astype(BF)
        for kv in range(2):
            for i in range(2):
                rows = pl.ds(pl.multiple_of((2 * i + 1 - c) * 128, 128), 128)
                remote(
                    gout.at[kv, zg, rows],
                    r1.at[kv, zg, pl.ds(i * 128, 128)],
                    e_ss.at[zg, kv * 2 + i],
                    e_rs.at[zg, kv * 2 + i],
                    sib,
                ).start()
        return 0

    lax.fori_loop(0, 4, grads, 0)

    dqs[...] = (dqt[...].T * inv).astype(BF)
    outs = []
    for h in range(2):
        outs.append(
            pltpu.make_async_copy(
                dqs.at[pl.ds(h * RESP, RESP)], o_rdq.at[0, :, pl.ds(h * HD, HD)], out_sem.at[h]
            )
        )
        outs.append(
            pltpu.make_async_copy(
                dqs.at[pl.ds(RL + h * PROWS, PROWS)], o_dq.at[:, pl.ds(h * HD, HD)], out_sem.at[2 + h]
            )
        )
    for cp in outs:
        cp.start()

    for k in range(4):
        zg = groups[k]
        for kv in range(2):
            for i in range(2):
                rows = pl.ds(pl.multiple_of((2 * i + 1 - c) * 128, 128), 128)
                remote(
                    gout.at[kv, zg, rows], r1.at[kv, zg, pl.ds(i * 128, 128)],
                    e_ss.at[zg, kv * 2 + i], e_rs.at[zg, kv * 2 + i], sib,
                ).wait()
    for zg in range(4):
        for i in range(2):
            zt = zg * 2 + i
            keep = pl.ds(pl.multiple_of((2 * i + c) * 128, 128), 128)
            got = pl.ds(i * 128, 128)
            both = gout[0, zg, keep, :].astype(F32) + r1[0, zg, got, :].astype(F32)
            both = both.astype(BF)
            for yy in range(NY):
                ady[yy, zt * 16 : (zt + 1) * 16, :] = both[yy * 16 : (yy + 1) * 16, :]
            both = gout[1, zg, keep, :].astype(F32) + r1[1, zg, got, :].astype(F32)
            adz[zt] = both.astype(BF)

    ycopies, zcopies = [], []
    for d in range(1, 8):
        yt = wrap(y + d, NY)
        cp = remote(ady.at[yt], ray.at[d], ya_ss.at[d], ya_rs.at[d], dev(x, yt, z, c))
        cp.start()
        ycopies.append(cp)
        zt = wrap(z + d, NZ)
        cp = remote(adz.at[zt], raz.at[d], za_ss.at[d], za_rs.at[d], dev(x, y, zt, c))
        cp.start()
        zcopies.append(cp)
    for cp in ycopies:
        cp.wait_recv()
    acc = ady[y].astype(F32)
    for d in range(1, 8):
        acc += ray[d].astype(F32)
    bdy[...] = acc.astype(BF)
    zb, yb = [], []
    for d in range(1, 8):
        zt = wrap(z + d, NZ)
        cp = remote(
            bdy.at[pl.ds(pl.multiple_of(zt * 16, 16), 16)], rbz.at[d], zb_ss.at[d], zb_rs.at[d], dev(x, y, zt, c)
        )
        cp.start()
        zb.append(cp)
    for cp in zcopies:
        cp.wait_recv()
    acc = adz[z].astype(F32)
    for d in range(1, 8):
        acc += raz[d].astype(F32)
    bdz[...] = acc.astype(BF)
    for d in range(1, 8):
        yt = wrap(y + d, NY)
        cp = remote(
            bdz.at[pl.ds(pl.multiple_of(yt * 16, 16), 16)], rby.at[d], yb_ss.at[d], yb_rs.at[d], dev(x, yt, z, c)
        )
        cp.start()
        yb.append(cp)
    for cp in zb:
        cp.wait_recv()
    acc = bdy[pl.ds(pl.multiple_of(z * 16, 16), 16), :].astype(F32)
    for d in range(1, 8):
        acc += rbz[d].astype(F32)
    fin[0:16, :] = acc.astype(BF)
    for cp in yb:
        cp.wait_recv()
    acc = bdz[pl.ds(pl.multiple_of(y * 16, 16), 16), :].astype(F32)
    for d in range(1, 8):
        acc += rby[d].astype(F32)
    fin[16:32, :] = acc.astype(BF)

    xo = 2 * zl + c
    zs, cs = x // 2, x % 2

    def final(i):
        zz, cc = i // 2, i % 2
        same = (xo == x) & (zl == zz) & (c == cc)
        return same, remote(fin, rfin.at[x], f_ss.at[i], f_rs.at[x], dev(xo, y, zh * 2 + zz, cc))

    for i in range(4):
        same, cp = final(i)

        @pl.when(jnp.logical_not(same))
        def _():
            cp.start()

        @pl.when(same)
        def _():
            rfin[x] = fin[...]

    for cp in gcopies:
        cp.wait_send()
    for k in range(1, 16):
        ps = wrap(p + k, 16)
        remote(rgr.at[ps], rgr.at[ps], g_ss.at[0], g_rs.at[ps], sib).wait_recv()
    for g in range(NX):
        acc = rgr[g * 4].astype(F32)
        for i in range(1, 4):
            acc += rgr[g * 4 + i].astype(F32)
        acc = acc.astype(BF)
        o_rdk[0, :, g * HD : (g + 1) * HD] = acc[0:16, :]
        o_rdv[0, :, g * HD : (g + 1) * HD] = acc[16:32, :]

    for xs in range(NX):
        mine = (x == xs) & (zs == zl) & (cs == c)

        @pl.when(jnp.logical_not(mine))
        def _():
            remote(fin, rfin.at[xs], f_ss.at[0], f_rs.at[xs], sib).wait_recv()

    place = zl * 2 + c
    for xs in range(NX):
        tile = rfin[xs].astype(F32)
        for half, out in ((0, o_dk), (16, o_dv)):
            rows = tile[half : half + 4, :]
            for i in range(1, 4):
                rows = jnp.where(place == i, tile[half + 4 * i : half + 4 * i + 4, :], rows)
            out[:, xs * HD : (xs + 1) * HD] = rows.astype(BF)

    for i in range(4):
        same, cp = final(i)

        @pl.when(jnp.logical_not(same))
        def _():
            cp.wait_send()

    for cp in pcopies + qcopies + dcopies + ycopies + zcopies + zb + yb:
        cp.wait_send()
    for cp in outs:
        cp.wait()


def shards(*args):
    hbm = pl.BlockSpec(memory_space=pl.ANY)
    smem = pl.BlockSpec(memory_space=pltpu.SMEM)
    vmem = pl.BlockSpec(memory_space=pltpu.VMEM)
    dma = pltpu.SemaphoreType.DMA
    shape = jax.ShapeDtypeStruct
    return pl.pallas_call(
        kernel,
        out_shape=(
            shape((PROWS, 256), BF),
            shape((4, 512), BF),
            shape((4, 512), BF),
            shape((1, RESP, 256), BF),
            shape((1, 16, 512), BF),
            shape((1, 16, 512), BF),
        ),
        in_specs=[hbm] * 5 + [smem] * 2 + [hbm] * 5 + [smem],
        out_specs=(hbm, vmem, vmem, hbm, vmem, vmem),
        scratch_shapes=[
            pltpu.VMEM((LANES, HD), BF),
            pltpu.VMEM((LANES, HD), BF),
            pltpu.VMEM((LANES, HD), BF),
            pltpu.VMEM((128, 512), BF),
            pltpu.VMEM((4, 128, HD), BF),
            pltpu.VMEM((2, 4, GROUP, HD), BF),
            pltpu.VMEM((4, 32, HD), BF),
            pltpu.VMEM((16, 32, HD), BF),
            pltpu.VMEM((RESP, HD), BF),
            pltpu.VMEM((RESP, HD), BF),
            pltpu.VMEM((4, GROUP, LANES), F32),
            pltpu.VMEM((RESP, RL), F32),
            pltpu.VMEM((LANES, HD), BF),
            pltpu.VMEM((HD, LANES), F32),
            pltpu.VMEM((2, 4, GROUP, HD), BF),
            pltpu.VMEM((2, 4, 256, HD), BF),
            pltpu.VMEM((8, 128, HD), BF),
            pltpu.VMEM((8, 128, HD), BF),
            pltpu.VMEM((8, 128, HD), BF),
            pltpu.VMEM((8, 128, HD), BF),
            pltpu.VMEM((128, HD), BF),
            pltpu.VMEM((128, HD), BF),
            pltpu.VMEM((8, 16, HD), BF),
            pltpu.VMEM((8, 16, HD), BF),
            pltpu.VMEM((32, HD), BF),
            pltpu.VMEM((4, 32, HD), BF),
            pltpu.VMEM((16, 32, HD), BF),
            pltpu.VMEM((16, 32, HD), BF),
            dma((13,)),
            dma((8,)),
            dma((4,)),
            dma((15,)),
            dma((16,)),
            dma((16,)),
            dma((16,)),
            dma((4,)),
            dma((4,)),
            dma((4, 4)),
            dma((4, 4)),
        ]
        + [dma((8,))] * 8
        + [dma((4,)), dma((4,)), dma((16,)), dma((16,))],
        compiler_params=pltpu.CompilerParams(
            collective_id=0, has_side_effects=True, vmem_limit_bytes=60 * 1024 * 1024
        ),
        name="attention_backward",
    )(*args)


def solution(mesh):
    wide = P("sample", "prompt")
    block = P("prompt", None)
    resp = P("sample", None, "prompt")
    near = P("sample", "prompt", None)
    owned = P(("prompt", "sample"), None)
    return jax.shard_map(
        shards,
        mesh=mesh,
        in_specs=(wide, wide, wide, block, block, block, block, resp, resp, resp, near, near, P("sample")),
        out_specs=(wide, owned, owned, resp, near, near),
        check_vma=False,
    )
```

time: 421 us -> 71.8 us (0.17)
  waiting for transfers between devices: 265 us -> 0 us
  Pallas kernels: 0 us -> 64.6 us
  blocking collectives: 48.2 us -> 0 us
  starting transfers between devices: 35.5 us -> 0 us
  matrix products: 21.9 us -> 0 us
  local copies, waits for them, and re-layouts: 24.4 us -> 5.57 us
  between operations: 15.8 us -> 1.31 us
  other arithmetic: 9.16 us -> 0 us
    unnamed x2 -> x0, waiting for transfers between devices: 229 us -> none
    pallas_call x0 -> x1, Pallas kernels: none -> 64.6 us  [shards(): pl.pallas_call(kernel, out_shape=(shape((PROWS, 256), BF), shape((4, 512)...]
    all_gather x1 -> x0, blocking collectives: 48.2 us -> none  [shards(): resp_every = lax.all_gather(resp_paired, 'prompt', axis=0, tiled=True)]
    all_to_all x3 -> x0, waiting for transfers between devices: 36.7 us -> none  [the longest x1 34.6 us: shards(): lax.all_to_all(prompt_terms.reshape(prompt_count, block_rows, 2 * HD), 'p...]
    all_to_all x3 -> x0, starting transfers between devices: 35.2 us -> none  [the longest x1 17.4 us: shards(): lax.all_to_all(resp_terms, 'prompt', split_axis=0, concat_axis=0, tiled=T...]
    dot_general x10 -> x0, matrix products: 21.9 us -> none  [the longest x2 7.82 us: one_head(): jnp.einsum('qk,qd->kd', weights, one_grad, preferred_element_type=jnp.flo...]
    reshape x7 -> x0, local copies, waits for them, and re-layouts: 5.82 us -> none  [the longest x2 2.43 us: join_heads(): summed = received.reshape(KVH, repeats, row_count, 2, HD).sum(axis=1)]
    reduce_sum x5 -> x0, other arithmetic: 5.65 us -> none  [the longest x2 3.8 us: softmax_rows(): return powers / jnp.sum(powers, axis=-1, keepdims=True)]
  transfers between devices with their start and end apart: 4 -> 0, of which waited for: 3 -> 0; matrix products, arithmetic and copies ran while one was open for 4% -> 0% of each run, Pallas kernels for 0% -> 0%
where the time goes in v1:
time: 71.8 us; the launch traced here: 71.4 us
  Pallas kernels  64.6 us (90%)
  local copies, waits for them, and re-layouts  5.57 us (8%)
  between operations  1.31 us (2%)
    pallas_call x1, Pallas kernels, shards(): pl.pallas_call(kernel, out_shape=(shape((PROWS, 256), BF), shape((4, 512)...  64.6 us
    unnamed x14, local copies, waits for them, and re-layouts  5.57 us

profile of v1, /device:TPU:1, one launch (start us, length us, event | category | flops | bytes accessed | tf_op | source)
XLA Modules:
  0.0 71.4 jit_solution(14440732176640492873)
XLA Ops:
  1.3 64.6 %attention_backward.1 = (bf16[64,256]{1,0:T(8,128)(2,1)}, bf16[4,512]{1,0:T(4,128)(2,1)}, bf16[4,512]{1,0:T(4,128)(2,1)}, bf16[1,256,256]{2,1,0:T(8,128)(2,1)}, ...) custom-call(bf16[64,256]{1,0:T(8,128)(2,1)} %pq.1, bf16[64,256]{1,0:T(8,128)(2,1)} %pg.1, bf16[64,256]{1,0:T(8,128)(2,1)} %po.1, ...), custom_call_target="tpu_custom_call" | custom-call | tf_op jit(solution)/shard_map/attention_backward/pallas_call | solution.py:420
  65.8 0.0 copy-start.3
  65.9 1.4 %copy.26 = bf16[64,256]{1,0:T(8,128)(2,1)} copy(bf16[64,256]{1,0:T(8,128)(2,1)} %get-tuple-element.12) | data formatting | bytes 65536
  67.2 0.0 copy-done.3
  67.2 0.0 copy-start.2
  67.2 0.6 copy.27
  67.8 0.1 copy-done.2
  67.9 0.6 copy.28
  68.5 0.0 copy-start.1
  68.5 1.6 %copy.29 = bf16[1,256,256]{2,1,0:T(8,128)(2,1)} copy(bf16[1,256,256]{2,1,0:T(8,128)(2,1)} %get-tuple-element.15) | data formatting | bytes 262144
  70.1 0.0 copy-done.1
  70.1 0.0 copy-start
  70.1 0.6 copy.30
  70.7 0.1 copy-done
  70.8 0.6 copy.31
Async XLA Ops:
  65.8 1.4 %copy-start.3 = (bf16[4,512]{1,0:T(4,128)(2,1)S(1)}, bf16[4,512]{1,0:T(4,128)(2,1)}, u32[]{:S(2)}) copy-start(bf16[4,512]{1,0:T(4,128)(2,1)} %get-tuple-element.13) | copy-start | bytes 12292
  67.2 0.7 copy-start.2
  68.5 1.6 %copy-start.1 = (bf16[1,16,512]{2,1,0:T(8,128)(2,1)S(1)}, bf16[1,16,512]{2,1,0:T(8,128)(2,1)}, u32[]{:S(2)}) copy-start(bf16[1,16,512]{2,1,0:T(8,128)(2,1)} %get-tuple-element.16) | copy-start | bytes 49156
  70.1 0.7 %copy-start = (bf16[1,16,512]{2,1,0:T(8,128)(2,1)S(1)}, bf16[1,16,512]{2,1,0:T(8,128)(2,1)}, u32[]{:S(2)}) copy-start(bf16[1,16,512]{2,1,0:T(8,128)(2,1)} %get-tuple-element.17) | copy-start | bytes 49156

commit v2 on v1

--- a/solution.py
+++ b/solution.py
@@ -21,6 +21,7 @@
 RL = 2 * RESP
 LANES = RL + 2 * PROWS
 GROUP = 512
+HALF = 64
 
 
 def dot_t(a, b):
@@ -41,7 +42,7 @@
     qm, gm, om, codes, deq, table, rsend, rtab, kr, vr, S, Sr, dqs, dqt,
     gout, r1, ady, adz, ray, raz, bdy, bdz, rby, rbz, fin, rfin, rgs, rgr,
     in_sem, rin_sem, out_sem,
-    p_ss, p_rs, q_ss, q_rs, d_ss, d_rs, e_ss, e_rs, ya_ss, ya_rs, za_ss, za_rs,
+    p_ss, p_rs, q_ss, q_rs, h_ss, h_rs, d_ss, d_rs, e_ss, e_rs, ya_ss, ya_rs, za_ss, za_rs,
     yb_ss, yb_rs, zb_ss, zb_rs, f_ss, f_rs, g_ss, g_rs,
 ):
     p = lax.axis_index("prompt")
@@ -50,6 +51,7 @@
     y, zl, c = s // 4, (s // 2) % 2, s % 2
     z = zh * 2 + zl
     sg = 2 * zl - 1
+    hy = y % 2
     inv = 1.0 / math.sqrt(HD)
 
     def dev(xx, yy, zz, cc):
@@ -117,24 +119,30 @@
             scale = jnp.where(c == 0, ks[b, g], vs[b, g])
             block = codes[b * SBLK : (b + 1) * SBLK, g * HD : (g + 1) * HD].astype(F32) * scale
             deq[g, b * SBLK : (b + 1) * SBLK, :] = block.astype(BF)
-    own_rows = pl.ds(pl.multiple_of(x * 128, 128), 128)
-    table[c, zh, own_rows, :] = deq[x]
+    own_rows = pl.ds(pl.multiple_of(x * HALF, HALF), HALF)
+    for half in range(2):
+        table[c, zh, half, own_rows, :] = deq[x, half * HALF : (half + 1) * HALF, :]
     for cp in rloads:
         cp.wait()
 
     pl.semaphore_wait(bar, len(partners))
 
-    psends = []
-    for d in (1, 2, 3):
-        for dx in range(NX):
-            psends.append((wrap(x + dx, NX), wrap(z + sg * d, NZ)))
-    for dx in (1, 2, 3):
-        psends.append((wrap(x + dx, NX), z))
     pcopies = []
-    for i, (xt, zt) in enumerate(psends):
-        cp = remote(deq.at[xt], table.at[c, zh, own_rows], p_ss.at[i], p_rs.at[p], dev(xt, y, zt, c))
+
+    def psend(xt, zt, half):
+        src = deq.at[xt, pl.ds(pl.multiple_of(half * HALF, HALF), HALF)]
+        cp = remote(
+            src, table.at[c, zh, half, own_rows], p_ss.at[len(pcopies)], p_rs.at[half, p], dev(xt, y, zt, c)
+        )
         cp.start()
         pcopies.append(cp)
+
+    for d in (3, 2, 1):
+        for dx in (2, 1, 3, 0):
+            psend(wrap(x + dx, NX), wrap(z + sg * d, NZ), hy)
+    for dx in (2, 1, 3):
+        for half in range(2):
+            psend(wrap(x + dx, NX), z, half)
     qcopies = []
     for k in range(1, 16):
         pt = wrap(p + k, 16)
@@ -145,18 +153,31 @@
 
     groups = [zh, wrap(zh + sg, NZH), wrap(zh - sg, NZH), wrap(zh + 2, NZH)]
 
-    dcopies = []
-    for k in range(4):
+    dcopies, hcopies = [], []
+
+    def hand(k, half, part, sem):
+        cp = remote(part, part, d_ss.at[k, half], d_rs.at[groups[k], sem], sib)
+        cp.start()
+        dcopies.append(cp)
+
+    for dx in (1, 3, 2):
+        xs = wrap(x + dx, NX)
+        rows = pl.ds(pl.multiple_of(xs * HALF, HALF), HALF)
+        for half in range(2):
+            piece = table.at[c, zh, half, rows]
+            remote(piece, piece, p_ss.at[0], p_rs.at[half, xs * 4 + zh], sib).wait_recv()
+    hand(0, 0, table.at[c, zh], 0)
+    for k in range(1, 4):
         zg = groups[k]
-        for dx in range(NX):
-            xs = wrap(x + dx, NX)
-            rows = pl.ds(pl.multiple_of(xs * 128, 128), 128)
-            piece = table.at[c, zg, rows]
-            if k or dx:
-                remote(piece, piece, p_ss.at[0], p_rs.at[xs * 4 + zg], sib).wait_recv()
-        cp = remote(table.at[c, zg], table.at[c, zg], d_ss.at[k], d_rs.at[zg], sib)
-        cp.start()
-        dcopies.append(cp)
+        for i in range(2):
+            for xs in (2 * i, 2 * i + 1):
+                piece = table.at[c, zg, hy, pl.ds(xs * HALF, HALF)]
+                remote(piece, piece, p_ss.at[0], p_rs.at[hy, xs * 4 + zg], sib).wait_recv()
+            part = table.at[c, zg, hy, pl.ds(i * 2 * HALF, 2 * HALF)]
+            cp = remote(part, part, h_ss.at[k - 1, i], h_rs.at[zg, i], dev(x, wrap(y + 1 - 2 * i, NY), z, c))
+            cp.start()
+            hcopies.append(cp)
+        hand(k, 0, table.at[c, zg, hy], hy)
 
     for cp in loads:
         cp.wait()
@@ -167,6 +188,13 @@
         gm[h * RESP : (h + 1) * RESP, :] = jnp.where(live, block, jnp.zeros_like(block))
     delta = jnp.sum((gm[...].astype(F32) * om[...].astype(F32)).T, axis=0, keepdims=True)
 
+    for k in range(1, 4):
+        zg = groups[k]
+        for i in range(2):
+            part = table.at[c, zg, 1 - hy, pl.ds(i * 2 * HALF, 2 * HALF)]
+            remote(part, part, h_ss.at[0, 0], h_rs.at[zg, i], sib).wait_recv()
+        hand(k, 1, table.at[c, zg, 1 - hy], 1 - hy)
+
     for k in range(1, 16):
         ps = wrap(p + k, 16)
         remote(rtab.at[ps], rtab.at[ps], q_ss.at[0], q_rs.at[ps], sib).wait_recv()
@@ -174,10 +202,12 @@
         kr[i * 16 : (i + 1) * 16, :] = rtab[i, 0:16, :]
         vr[i * 16 : (i + 1) * 16, :] = rtab[i, 16:32, :]
 
-    for k in range(4):
-        zg = groups[k]
-        other = table.at[1 - c, zg]
-        remote(other, other, d_ss.at[0], d_rs.at[zg], sib).wait_recv()
+    other = table.at[1 - c, zh]
+    remote(other, other, d_ss.at[0, 0], d_rs.at[zh, 0], sib).wait_recv()
+    for k in range(1, 4):
+        for half in range(2):
+            other = table.at[1 - c, groups[k], half]
+            remote(other, other, d_ss.at[0, 0], d_rs.at[groups[k], half], sib).wait_recv()
 
     u = lax.broadcasted_iota(jnp.int32, (RESP, RESP), 0)
     t = lax.broadcasted_iota(jnp.int32, (RESP, RESP), 1)
@@ -196,12 +226,12 @@
 
     def scores(k, top):
         zg = group_of(k)
-        keys = table[0, zg]
+        keys = table[0, zg].reshape(GROUP, HD)
         far = dot_t(keys, qm[0:RL, :])
         S[zg, :, 0:RL] = far
         row = lax.broadcasted_iota(jnp.int32, (GROUP, 2 * PROWS), 0)
         lane = lax.broadcasted_iota(jnp.int32, (GROUP, 2 * PROWS), 1)
-        place = (row // 128) * 512 + zg * 128 + row % 128
+        place = ((row // HALF) % NX) * GROUP + zg * 128 + (row // 256) * HALF + row % HALF
         own = dot_t(keys, qm[RL:LANES, :])
         own = jnp.where(place <= s * PROWS + lane % PROWS, own, NEG)
         S[zg, :, RL:LANES] = own
@@ -241,27 +271,72 @@
         gcopies.append(cp)
     rgr[p] = rgs[p]
 
+    def pair(zg, kv, i):
+        rows = pl.ds(pl.multiple_of((2 * i + 1 - c) * 128, 128), 128)
+        got = r1.at[kv, zg, pl.ds(i * 128, 128)]
+        return remote(gout.at[kv, zg, rows], got, e_ss.at[zg, kv * 2 + i], e_rs.at[zg, kv * 2 + i], sib)
+
+    def ysend(zg, d):
+        yt = wrap(y + d, NY)
+        rows = pl.ds(pl.multiple_of(zg * 32, 32), 32)
+        return remote(ady.at[yt, rows], ray.at[d, rows], ya_ss.at[zg, d], ya_rs.at[zg, d], dev(x, yt, z, c))
+
+    def zsend(zt):
+        return remote(adz.at[zt], raz.at[z], za_ss.at[zt], za_rs.at[z], dev(x, y, zt, c))
+
+    def spread(k):
+        zg = group_of(k)
+        for kv in range(2):
+            for i in range(2):
+                pair(zg, kv, i).wait_recv()
+        for i in range(2):
+            zt = zg * 2 + i
+            keep = pl.ds(pl.multiple_of((2 * i + c) * 128, 128), 128)
+            got = pl.ds(i * 128, 128)
+            both = gout[0, zg, keep, :].astype(F32) + r1[0, zg, got, :].astype(F32)
+            both = both.astype(BF)
+            rows = pl.ds(pl.multiple_of(zt * 16, 16), 16)
+            for yy in range(NY):
+                ady[yy, rows, :] = both[yy * 16 : (yy + 1) * 16, :]
+            both = gout[1, zg, keep, :].astype(F32) + r1[1, zg, got, :].astype(F32)
+            adz[zt] = both.astype(BF)
+        for d in (4, 3, 5, 2, 6, 1, 7):
+            ysend(zg, d).start()
+        for i in range(2):
+            zt = zg * 2 + i
+
+            @pl.when(zt != z)
+            def _():
+                zsend(zt).start()
+
     def grads(k, _):
         zg = group_of(k)
         prob = S[zg] * rtotal
-        dp = dot_t(table[1, zg], gm[...])
+        dp = dot_t(table[1, zg].reshape(GROUP, HD), gm[...])
         ds = (prob * (dp - delta)).astype(BF)
-        dqt[...] += dot_l(table[0, zg], ds)
-        gout[0, zg] = (dot_n(ds, qm[...]) * inv).astype(BF)
-        gout[1, zg] = dot_n(prob.astype(BF), gm[...]).astype(BF)
+        dqt[...] += dot_l(table[0, zg].reshape(GROUP, HD), ds)
+        for kv in range(2):
+            if kv == 0:
+                sums = (dot_n(ds, qm[...]) * inv).astype(BF)
+            else:
+                sums = dot_n(prob.astype(BF), gm[...]).astype(BF)
+            for half in range(2):
+                for xs in range(NX):
+                    start = half * 256 + xs * HALF
+                    to = xs * 128 + half * HALF
+                    gout[kv, zg, to : to + HALF, :] = sums[start : start + HALF, :]
         for kv in range(2):
             for i in range(2):
-                rows = pl.ds(pl.multiple_of((2 * i + 1 - c) * 128, 128), 128)
-                remote(
-                    gout.at[kv, zg, rows],
-                    r1.at[kv, zg, pl.ds(i * 128, 128)],
-                    e_ss.at[zg, kv * 2 + i],
-                    e_rs.at[zg, kv * 2 + i],
-                    sib,
-                ).start()
+                pair(zg, kv, i).start()
+
+        @pl.when(k > 0)
+        def _():
+            spread(k - 1)
+
         return 0
 
     lax.fori_loop(0, 4, grads, 0)
+    spread(3)
 
     dqs[...] = (dqt[...].T * inv).astype(BF)
     outs = []
@@ -279,39 +354,9 @@
     for cp in outs:
         cp.start()
 
-    for k in range(4):
-        zg = groups[k]
-        for kv in range(2):
-            for i in range(2):
-                rows = pl.ds(pl.multiple_of((2 * i + 1 - c) * 128, 128), 128)
-                remote(
-                    gout.at[kv, zg, rows], r1.at[kv, zg, pl.ds(i * 128, 128)],
-                    e_ss.at[zg, kv * 2 + i], e_rs.at[zg, kv * 2 + i], sib,
-                ).wait()
     for zg in range(4):
-        for i in range(2):
-            zt = zg * 2 + i
-            keep = pl.ds(pl.multiple_of((2 * i + c) * 128, 128), 128)
-            got = pl.ds(i * 128, 128)
-            both = gout[0, zg, keep, :].astype(F32) + r1[0, zg, got, :].astype(F32)
-            both = both.astype(BF)
-            for yy in range(NY):
-                ady[yy, zt * 16 : (zt + 1) * 16, :] = both[yy * 16 : (yy + 1) * 16, :]
-            both = gout[1, zg, keep, :].astype(F32) + r1[1, zg, got, :].astype(F32)
-            adz[zt] = both.astype(BF)
-
-    ycopies, zcopies = [], []
-    for d in range(1, 8):
-        yt = wrap(y + d, NY)
-        cp = remote(ady.at[yt], ray.at[d], ya_ss.at[d], ya_rs.at[d], dev(x, yt, z, c))
-        cp.start()
-        ycopies.append(cp)
-        zt = wrap(z + d, NZ)
-        cp = remote(adz.at[zt], raz.at[d], za_ss.at[d], za_rs.at[d], dev(x, y, zt, c))
-        cp.start()
-        zcopies.append(cp)
-    for cp in ycopies:
-        cp.wait_recv()
+        for d in range(1, 8):
+            ysend(zg, d).wait_recv()
     acc = ady[y].astype(F32)
     for d in range(1, 8):
         acc += ray[d].astype(F32)
@@ -324,11 +369,12 @@
         )
         cp.start()
         zb.append(cp)
-    for cp in zcopies:
-        cp.wait_recv()
+    for d in range(1, 8):
+        zs = wrap(z + d, NZ)
+        remote(adz.at[zs], raz.at[zs], za_ss.at[0], za_rs.at[zs], sib).wait_recv()
     acc = adz[z].astype(F32)
     for d in range(1, 8):
-        acc += raz[d].astype(F32)
+        acc += raz[wrap(z + d, NZ)].astype(F32)
     bdz[...] = acc.astype(BF)
     for d in range(1, 8):
         yt = wrap(y + d, NY)
@@ -337,38 +383,6 @@
         )
         cp.start()
         yb.append(cp)
-    for cp in zb:
-        cp.wait_recv()
-    acc = bdy[pl.ds(pl.multiple_of(z * 16, 16), 16), :].astype(F32)
-    for d in range(1, 8):
-        acc += rbz[d].astype(F32)
-    fin[0:16, :] = acc.astype(BF)
-    for cp in yb:
-        cp.wait_recv()
-    acc = bdz[pl.ds(pl.multiple_of(y * 16, 16), 16), :].astype(F32)
-    for d in range(1, 8):
-        acc += rby[d].astype(F32)
-    fin[16:32, :] = acc.astype(BF)
-
-    xo = 2 * zl + c
-    zs, cs = x // 2, x % 2
-
-    def final(i):
-        zz, cc = i // 2, i % 2
-        same = (xo == x) & (zl == zz) & (c == cc)
-        return same, remote(fin, rfin.at[x], f_ss.at[i], f_rs.at[x], dev(xo, y, zh * 2 + zz, cc))
-
-    for i in range(4):
-        same, cp = final(i)
-
-        @pl.when(jnp.logical_not(same))
-        def _():
-            cp.start()
-
-        @pl.when(same)
-        def _():
-            rfin[x] = fin[...]
-
     for cp in gcopies:
         cp.wait_send()
     for k in range(1, 16):
@@ -382,20 +396,52 @@
         o_rdk[0, :, g * HD : (g + 1) * HD] = acc[0:16, :]
         o_rdv[0, :, g * HD : (g + 1) * HD] = acc[16:32, :]
 
+    for cp in zb:
+        cp.wait_recv()
+    acc = bdy[pl.ds(pl.multiple_of(z * 16, 16), 16), :].astype(F32)
+    for d in range(1, 8):
+        acc += rbz[d].astype(F32)
+    fin[0:16, :] = acc.astype(BF)
+    for cp in yb:
+        cp.wait_recv()
+    acc = bdz[pl.ds(pl.multiple_of(y * 16, 16), 16), :].astype(F32)
+    for d in range(1, 8):
+        acc += rby[d].astype(F32)
+    fin[16:32, :] = acc.astype(BF)
+
+    xo = 2 * zl + c
+    zf, cf = x // 2, x % 2
+
+    def final(i):
+        zz, cc = i // 2, i % 2
+        same = (xo == x) & (zl == zz) & (c == cc)
+        return same, remote(fin, rfin.at[x], f_ss.at[i], f_rs.at[x], dev(xo, y, zh * 2 + zz, cc))
+
+    for i in range(4):
+        same, cp = final(i)
+
+        @pl.when(jnp.logical_not(same))
+        def _():
+            cp.start()
+
+        @pl.when(same)
+        def _():
+            rfin[x] = fin[...]
+
     for xs in range(NX):
-        mine = (x == xs) & (zs == zl) & (cs == c)
+        mine = (x == xs) & (zf == zl) & (cf == c)
 
         @pl.when(jnp.logical_not(mine))
         def _():
             remote(fin, rfin.at[xs], f_ss.at[0], f_rs.at[xs], sib).wait_recv()
 
-    place = zl * 2 + c
+    spot = zl * 2 + c
     for xs in range(NX):
         tile = rfin[xs].astype(F32)
         for half, out in ((0, o_dk), (16, o_dv)):
             rows = tile[half : half + 4, :]
             for i in range(1, 4):
-                rows = jnp.where(place == i, tile[half + 4 * i : half + 4 * i + 4, :], rows)
+                rows = jnp.where(spot == i, tile[half + 4 * i : half + 4 * i + 4, :], rows)
             out[:, xs * HD : (xs + 1) * HD] = rows.astype(BF)
 
     for i in range(4):
@@ -405,10 +451,23 @@
         def _():
             cp.wait_send()
 
-    for cp in pcopies + qcopies + dcopies + ycopies + zcopies + zb + yb:
+    for cp in pcopies + qcopies + hcopies + dcopies + zb + yb:
         cp.wait_send()
+    for zg in range(4):
+        for kv in range(2):
+            for i in range(2):
+                pair(zg, kv, i).wait_send()
+        for d in range(1, 8):
+            ysend(zg, d).wait_send()
+    for d in range(1, 8):
+        zsend(wrap(z + d, NZ)).wait_send()
     for cp in outs:
         cp.wait()
+
+
+def place(*refs):
+    for i in range(6):
+        refs[6 + i][...] = refs[i][...]
 
 
 def shards(*args):
@@ -417,7 +476,7 @@
     vmem = pl.BlockSpec(memory_space=pltpu.VMEM)
     dma = pltpu.SemaphoreType.DMA
     shape = jax.ShapeDtypeStruct
-    return pl.pallas_call(
+    made = pl.pallas_call(
         kernel,
         out_shape=(
             shape((PROWS, 256), BF),
@@ -435,7 +494,7 @@
             pltpu.VMEM((LANES, HD), BF),
             pltpu.VMEM((128, 512), BF),
             pltpu.VMEM((4, 128, HD), BF),
-            pltpu.VMEM((2, 4, GROUP, HD), BF),
+            pltpu.VMEM((2, 4, 2, GROUP // 2, HD), BF),
             pltpu.VMEM((4, 32, HD), BF),
             pltpu.VMEM((16, 32, HD), BF),
             pltpu.VMEM((RESP, HD), BF),
@@ -461,22 +520,34 @@
             dma((13,)),
             dma((8,)),
             dma((4,)),
-            dma((15,)),
+            dma((18,)),
+            dma((2, 16)),
             dma((16,)),
             dma((16,)),
-            dma((16,)),
-            dma((4,)),
-            dma((4,)),
+            dma((3, 2)),
+            dma((4, 2)),
+            dma((4, 2)),
+            dma((4, 2)),
             dma((4, 4)),
             dma((4, 4)),
+            dma((4, 8)),
+            dma((4, 8)),
         ]
-        + [dma((8,))] * 8
+        + [dma((8,))] * 6
         + [dma((4,)), dma((4,)), dma((16,)), dma((16,))],
         compiler_params=pltpu.CompilerParams(
             collective_id=0, has_side_effects=True, vmem_limit_bytes=60 * 1024 * 1024
         ),
         name="attention_backward",
     )(*args)
+    return pl.pallas_call(
+        place,
+        out_shape=tuple(shape(a.shape, a.dtype) for a in made),
+        in_specs=[vmem] * 6,
+        out_specs=[vmem] * 6,
+        compiler_params=pltpu.CompilerParams(vmem_limit_bytes=60 * 1024 * 1024),
+        name="place_outputs",
+    )(*made)
 
 
 def solution(mesh):

time: 71.8 us -> 63.6 us (0.89)
  local copies, waits for them, and re-layouts: 5.57 us -> 0 us
  Pallas kernels: 64.6 us -> 62.1 us
    unnamed x14 -> x0, local copies, waits for them, and re-layouts: 5.57 us -> none
    pallas_call x1, Pallas kernels: 64.6 us -> 60.5 us  [shards(): pl.pallas_call(kernel, out_shape=(shape((PROWS, 256), BF), shape((4, 512)...]
    pallas_call x0 -> x1, Pallas kernels: none -> 1.6 us  [shards(): pl.pallas_call(place, out_shape=tuple((shape(a.shape, a.dtype) for a in m...]
where the time goes in v2:
time: 63.6 us; the launch traced here: 63.4 us
  Pallas kernels  62.1 us (98%)
  between operations  1.29 us (2%)
    pallas_call x1, Pallas kernels, shards(): pl.pallas_call(kernel, out_shape=(shape((PROWS, 256), BF), shape((4, 512)...  60.5 us
    pallas_call x1, Pallas kernels, shards(): pl.pallas_call(place, out_shape=tuple((shape(a.shape, a.dtype) for a in m...  1.6 us

profile of v2, /device:TPU:1, one launch (start us, length us, event | category | flops | bytes accessed | tf_op | source)
XLA Modules:
  0.0 63.4 jit_solution(1305594512733937703)
XLA Ops:
  1.3 60.5 %attention_backward.1 = (bf16[64,256]{1,0:T(8,128)(2,1)}, bf16[4,512]{1,0:T(4,128)(2,1)}, bf16[4,512]{1,0:T(4,128)(2,1)}, bf16[1,256,256]{2,1,0:T(8,128)(2,1)}, ...) custom-call(bf16[64,256]{1,0:T(8,128)(2,1)} %pq.1, bf16[64,256]{1,0:T(8,128)(2,1)} %pg.1, bf16[64,256]{1,0:T(8,128)(2,1)} %po.1, ...), custom_call_target="tpu_custom_call" | custom-call | tf_op jit(solution)/shard_map/attention_backward/pallas_call | solution.py:479
  61.8 1.6 %place_outputs.1 = (bf16[64,256]{1,0:T(8,128)(2,1)}, bf16[4,512]{1,0:T(4,128)(2,1)}, bf16[4,512]{1,0:T(4,128)(2,1)}, bf16[1,256,256]{2,1,0:T(8,128)(2,1)}, bf16[...) custom-call(bf16[64,256]{1,0:T(8,128)(2,1)} %get-tuple-element.12.refs_0_, bf16[4,512]{1,0:T(4,128)(2,1)} %get-tuple-element.13.refs_1_, ...), custom_call_target="tpu_custom_call" | custom-call | tf_op jit(solution)/shard_map/place_outputs/pallas_call | solution.py:543

commit v3 on v2

v3 whole, which is shorter than its diff:
```python
import math

import jax
import jax.numpy as jnp
from jax import lax
from jax.experimental import pallas as pl
from jax.experimental.pallas import tpu as pltpu
from jax.sharding import PartitionSpec as P

HD = 128
SBLK = 32
MESH = pl.DeviceIdType.MESH
NEG = -1e30
F32 = jnp.float32
BF = jnp.bfloat16
LOG2E = 1.4426950408889634

NX, NY, NZ, NZH = 4, 8, 8, 4
RESP = 256
PROWS = 64
RL = 2 * RESP
LANES = RL + 2 * PROWS
GROUP = 512
HALF = 64


def dot_t(a, b):
    return lax.dot_general(a, b, (((1,), (1,)), ((), ())), preferred_element_type=F32)


def dot_n(a, b):
    return lax.dot_general(a, b, (((1,), (0,)), ((), ())), preferred_element_type=F32)


def dot_l(a, b):
    return lax.dot_general(a, b, (((0,), (0,)), ((), ())), preferred_element_type=F32)


def kernel(
    pq, pg, po, kc, vc, ks, vs, rq, rg, ro, rk, rv, ln,
    o_dq, o_dk, o_dv, o_rdq, o_rdk, o_rdv,
    qm, gm, om, codes, deq, table, rsend, rtab, kr, vr, S, Sr, dqs, dqt,
    mx, sm, gout, r1, ady, adz, ray, raz, bdy, bdz, rby, rbz, fin, rfin, rgs, rgr, scl, lens,
    in_sem,
    p_ss, p_rs, q_ss, q_rs, h_ss, h_rs, d_ss, d_rs, e_ss, e_rs, ya_ss, ya_rs, za_ss, za_rs,
    yb_ss, yb_rs, zb_ss, zb_rs, f_ss, f_rs, g_ss, g_rs,
):
    p = lax.axis_index("prompt")
    s = lax.axis_index("sample")
    x, zh = p // 4, p % 4
    y, zl, c = s // 4, (s // 2) % 2, s % 2
    z = zh * 2 + zl
    sg = 2 * zl - 1
    hy = y % 2
    inv = 1.0 / math.sqrt(HD)

    def dev(xx, yy, zz, cc):
        return (xx * 4 + zz // 2, yy * 4 + (zz % 2) * 2 + cc)

    def wrap(v, n):
        return lax.rem(v + 2 * n, n)

    def remote(src, dst, ss, rs, to):
        return pltpu.make_async_remote_copy(src, dst, ss, rs, device_id=to, device_id_type=MESH)

    sib = dev(x, y, z, 1 - c)

    bar = pltpu.get_barrier_semaphore()
    partners = []
    for dx in range(NX):
        for dz in range(NZ):
            if dx or dz:
                partners.append(dev(wrap(x + dx, NX), y, wrap(z + dz, NZ), c))
    for dy in range(1, NY):
        partners.append(dev(x, wrap(y + dy, NY), z, c))
    for dx in range(NX):
        for zz in range(2):
            partners.append(dev(wrap(x + dx, NX), y, zh * 2 + zz, 1 - c))
    for to in partners:
        pl.semaphore_signal(bar, inc=1, device_id=to, device_id_type=MESH)

    def share(codes_ref, scale_ref):
        pltpu.make_async_copy(codes_ref, codes, in_sem.at[0]).start()
        pltpu.make_async_copy(scale_ref, scl, in_sem.at[1]).start()

    @pl.when(c == 0)
    def _():
        share(kc, ks)

    @pl.when(c == 1)
    def _():
        share(vc, vs)

    pltpu.make_async_copy(ln, lens, in_sem.at[2]).start()
    rloads = []
    for g in range(NX):
        for i, ref in enumerate((rk, rv)):
            rloads.append(
                pltpu.make_async_copy(
                    ref.at[0, :, pl.ds(g * HD, HD)], rsend.at[g, pl.ds(16 * i, 16)], in_sem.at[3]
                )
            )
    for cp in rloads:
        cp.start()
    loads = []
    for i, (pref, rref, dst) in enumerate(((pq, rq, qm), (pg, rg, gm), (po, ro, om))):
        for h in range(2):
            loads.append(
                pltpu.make_async_copy(
                    rref.at[0, :, pl.ds(h * HD, HD)], dst.at[pl.ds(h * RESP, RESP)], in_sem.at[4 + i]
                )
            )
            loads.append(
                pltpu.make_async_copy(
                    pref.at[:, pl.ds(h * HD, HD)], dst.at[pl.ds(RL + h * PROWS, PROWS)], in_sem.at[4 + i]
                )
            )
    for cp in loads:
        cp.start()

    pltpu.make_async_copy(kc, codes, in_sem.at[0]).wait()
    pltpu.make_async_copy(ks, scl, in_sem.at[1]).wait()
    for g in range(NX):
        for b in range(128 // SBLK):
            block = codes[b * SBLK : (b + 1) * SBLK, g * HD : (g + 1) * HD].astype(F32) * scl[b, g]
            deq[g, b * SBLK : (b + 1) * SBLK, :] = block.astype(BF)
    own_rows = pl.ds(pl.multiple_of(x * HALF, HALF), HALF)
    for half in range(2):
        table[c, zh, half, own_rows, :] = deq[x, half * HALF : (half + 1) * HALF, :]
    pltpu.make_async_copy(rsend, rsend, in_sem.at[3]).wait()

    pl.semaphore_wait(bar, len(partners))

    def psend(xt, zt, half, sem):
        src = deq.at[xt, pl.ds(pl.multiple_of(half * HALF, HALF), HALF)]
        remote(src, table.at[c, zh, half, own_rows], p_ss.at[0], sem, dev(xt, y, zt, c)).start()

    for d in (1, 2, 3):
        for dx in (2, 1, 3, 0):
            psend(wrap(x + dx, NX), wrap(z + sg * d, NZ), hy, p_rs.at[zh, x // 2])
    for dx in (2, 1, 3):
        for half in range(2):
            psend(wrap(x + dx, NX), z, half, p_rs.at[4, 0])
    for k in range(1, 16):
        pt = wrap(p + k, 16)
        remote(rsend.at[pt // 4], rtab.at[p], q_ss.at[0], q_rs.at[0], (pt, s)).start()
    rtab[p] = rsend[x]

    groups = [zh, wrap(zh + sg, NZH), wrap(zh - sg, NZH), wrap(zh + 2, NZH)]

    for i, dst in enumerate((qm, gm, om)):
        pltpu.make_async_copy(dst, dst, in_sem.at[4 + i]).wait()
    pltpu.make_async_copy(ln, lens, in_sem.at[2]).wait()
    length = lens[0]
    live = lax.broadcasted_iota(jnp.int32, (RESP, HD), 0) < length
    for h in range(2):
        block = gm[h * RESP : (h + 1) * RESP, :]
        gm[h * RESP : (h + 1) * RESP, :] = jnp.where(live, block, jnp.zeros_like(block))
    delta = jnp.sum((gm[...].astype(F32) * om[...].astype(F32)).T, axis=0, keepdims=True)

    def hand(k, part):
        remote(part, part, d_ss.at[0], d_rs.at[groups[k]], sib).start()

    def take_near():
        part = deq.at[pl.ds(0, 3)]
        remote(part, part, p_ss.at[0], p_rs.at[4, 0], sib).wait_recv()
        hand(0, table.at[c, zh])

    def take_far(k):
        zg = groups[k]
        for i in range(2):
            part = table.at[c, zg, hy, pl.ds(i * 2 * HALF, 2 * HALF)]
            remote(part, part, p_ss.at[0], p_rs.at[zg, i], sib).wait_recv()
            remote(part, part, h_ss.at[0], h_rs.at[zg, i], dev(x, wrap(y + 1 - 2 * i, NY), z, c)).start()
        hand(k, table.at[c, zg, hy])

    def take_beside(k):
        zg = groups[k]
        for i in range(2):
            part = table.at[c, zg, 1 - hy, pl.ds(i * 2 * HALF, 2 * HALF)]
            remote(part, part, h_ss.at[0], h_rs.at[zg, i], sib).wait_recv()
        hand(k, table.at[c, zg, 1 - hy])

    def group_of(k):
        step = jnp.where(k == 1, sg, jnp.where(k == 2, -sg, jnp.where(k == 3, 2, 0)))
        return lax.rem(zh + step + 4, 4)

    def absorb(k):
        zg = group_of(k)
        other = table.at[1 - c, zg]
        remote(other, other, d_ss.at[0], d_rs.at[zg], sib).wait_recv()
        keys = table[0, zg].reshape(GROUP, HD)
        far = dot_t(keys, qm[0:RL, :])
        best = jnp.max(far, axis=0, keepdims=True)
        mx[zg, :, 0:RL] = best
        far = jnp.exp2((far - best) * (inv * LOG2E))
        sm[zg, :, 0:RL] = jnp.sum(far, axis=0, keepdims=True)
        S[zg, :, 0:RL] = far
        row = lax.broadcasted_iota(jnp.int32, (GROUP, 2 * PROWS), 0)
        lane = lax.broadcasted_iota(jnp.int32, (GROUP, 2 * PROWS), 1)
        place = ((row // HALF) % NX) * GROUP + zg * 128 + (row // 256) * HALF + row % HALF
        own = dot_t(keys, qm[RL:LANES, :])
        own = jnp.where(place <= s * PROWS + lane % PROWS, own, NEG)
        best = jnp.max(own, axis=0, keepdims=True)
        mx[zg, :, RL:LANES] = best
        own = jnp.exp2((own - best) * (inv * LOG2E))
        sm[zg, :, RL:LANES] = jnp.sum(own, axis=0, keepdims=True)
        S[zg, :, RL:LANES] = own

    take_near()
    take_far(1)
    absorb(0)
    take_far(2)
    take_far(3)
    take_beside(1)
    take_beside(2)
    take_beside(3)

    def absorb_loop(k, _):
        absorb(k)
        return 0

    lax.fori_loop(1, 4, absorb_loop, 0)

    part = rtab.at[pl.ds(0, 15)]
    remote(part, part, q_ss.at[0], q_rs.at[0], sib).wait_recv()
    for i in range(16):
        kr[i * 16 : (i + 1) * 16, :] = rtab[i, 0:16, :]
        vr[i * 16 : (i + 1) * 16, :] = rtab[i, 16:32, :]
    u = lax.broadcasted_iota(jnp.int32, (RESP, RESP), 0)
    t = lax.broadcasted_iota(jnp.int32, (RESP, RESP), 1)
    near = (u <= t) & (u < length)
    sr = dot_t(kr[...], qm[0:RL, :])
    tops, sums = [], []
    for h in range(2):
        part = jnp.where(near, sr[:, h * RESP : (h + 1) * RESP], NEG)
        best = jnp.max(part, axis=0, keepdims=True)
        part = jnp.exp2((part - best) * (inv * LOG2E))
        Sr[:, h * RESP : (h + 1) * RESP] = part
        tops.append(best)
        sums.append(jnp.sum(part, axis=0, keepdims=True))
    tops = jnp.concatenate(tops + [jnp.full((1, 2 * PROWS), NEG, F32)], axis=1)
    sums = jnp.concatenate(sums + [jnp.zeros((1, 2 * PROWS), F32)], axis=1)

    top = tops
    for zg in range(4):
        top = jnp.maximum(top, mx[zg])
    rscale = jnp.exp2((tops - top) * (inv * LOG2E))
    total = sums * rscale
    scales = []
    for zg in range(4):
        scale = jnp.exp2((mx[zg] - top) * (inv * LOG2E))
        total += sm[zg] * scale
        scales.append(scale)
    rtotal = 1.0 / total
    rscale = rscale * rtotal
    for zg in range(4):
        mx[zg] = scales[zg] * rtotal

    def pair(zg, kv, i):
        rows = pl.ds(pl.multiple_of((2 * i + 1 - c) * 128, 128), 128)
        got = r1.at[kv, zg, pl.ds(i * 128, 128)]
        return remote(gout.at[kv, zg, rows], got, e_ss.at[0], e_rs.at[zg], sib)

    def ysend(zg, d):
        yt = wrap(y + d, NY)
        rows = pl.ds(pl.multiple_of(zg * 32, 32), 32)
        return remote(ady.at[yt, rows], ray.at[d, rows], ya_ss.at[0], ya_rs.at[0], dev(x, yt, z, c))

    def zsend(zt):
        return remote(adz.at[zt], raz.at[z], za_ss.at[0], za_rs.at[0], dev(x, y, zt, c))

    def spread(k):
        zg = group_of(k)
        part = gout.at[0, zg]
        remote(part, part, e_ss.at[0], e_rs.at[zg], sib).wait_recv()
        for i in range(2):
            zt = zg * 2 + i
            keep = pl.ds(pl.multiple_of((2 * i + c) * 128, 128), 128)
            got = pl.ds(i * 128, 128)
            both = gout[0, zg, keep, :].astype(F32) + r1[0, zg, got, :].astype(F32)
            both = both.astype(BF)
            rows = pl.ds(pl.multiple_of(zt * 16, 16), 16)
            for yy in range(NY):
                ady[yy, rows, :] = both[yy * 16 : (yy + 1) * 16, :]
            both = gout[1, zg, keep, :].astype(F32) + r1[1, zg, got, :].astype(F32)
            adz[zt] = both.astype(BF)
        for d in (4, 3, 5, 2, 6, 1, 7):
            ysend(zg, d).start()
        for i in range(2):
            zt = zg * 2 + i

            @pl.when(zt != z)
            def _():
                zsend(zt).start()

    def grads(k, _):
        zg = group_of(k)
        prob = S[zg] * mx[zg]
        dp = dot_t(table[1, zg].reshape(GROUP, HD), gm[...])
        ds = (prob * (dp - delta)).astype(BF)
        dqt[...] += dot_l(table[0, zg].reshape(GROUP, HD), ds)
        for kv in range(2):
            if kv == 0:
                sums = (dot_n(ds, qm[...]) * inv).astype(BF)
            else:
                sums = dot_n(prob.astype(BF), gm[...]).astype(BF)
            for half in range(2):
                for xs in range(NX):
                    start = half * 256 + xs * HALF
                    to = xs * 128 + half * HALF
                    gout[kv, zg, to : to + HALF, :] = sums[start : start + HALF, :]
        for kv in range(2):
            for i in range(2):
                pair(zg, kv, i).start()

        @pl.when(k > 0)
        def _():
            spread(k - 1)

        return 0

    dqt[...] = jnp.zeros_like(dqt)
    lax.fori_loop(0, 4, grads, 0)

    prob = Sr[...] * rscale[:, 0:RL]
    dp = dot_t(vr[...], gm[0:RL, :])
    ds = (prob * (dp - delta[:, 0:RL])).astype(BF)
    dqt[:, 0:RL] += dot_l(kr[...], ds)
    dkr = (dot_n(ds, qm[0:RL, :]) * inv).astype(BF)
    dvr = dot_n(prob.astype(BF), gm[0:RL, :]).astype(BF)
    for i in range(16):
        rgs[i, 0:16, :] = dkr[i * 16 : (i + 1) * 16, :]
        rgs[i, 16:32, :] = dvr[i * 16 : (i + 1) * 16, :]
    spread(3)
    for k in range(1, 16):
        pt = wrap(p + k, 16)
        remote(rgs.at[pt], rgr.at[p], g_ss.at[0], g_rs.at[0], (pt, s)).start()
    rgr[p] = rgs[p]

    dqs[...] = (dqt[...].T * inv).astype(BF)
    outs = []
    for h in range(2):
        outs.append(
            pltpu.make_async_copy(
                dqs.at[pl.ds(h * RESP, RESP)], o_rdq.at[0, :, pl.ds(h * HD, HD)], in_sem.at[7]
            )
        )
        outs.append(
            pltpu.make_async_copy(
                dqs.at[pl.ds(RL + h * PROWS, PROWS)], o_dq.at[:, pl.ds(h * HD, HD)], in_sem.at[7]
            )
        )
    for cp in outs:
        cp.start()

    seven = ray.at[pl.ds(1, 7)]
    remote(seven, seven, ya_ss.at[0], ya_rs.at[0], sib).wait_recv()
    acc = ady[y].astype(F32)
    for d in range(1, 8):
        acc += ray[d].astype(F32)
    bdy[...] = acc.astype(BF)
    for d in range(1, 8):
        zt = wrap(z + d, NZ)
        cp = remote(
            bdy.at[pl.ds(pl.multiple_of(zt * 16, 16), 16)], rbz.at[d], zb_ss.at[0], zb_rs.at[0], dev(x, y, zt, c)
        )
        cp.start()
    remote(seven, seven, za_ss.at[0], za_rs.at[0], sib).wait_recv()
    acc = adz[z].astype(F32)
    for d in range(1, 8):
        acc += raz[wrap(z + d, NZ)].astype(F32)
    bdz[...] = acc.astype(BF)
    for d in range(1, 8):
        yt = wrap(y + d, NY)
        cp = remote(
            bdz.at[pl.ds(pl.multiple_of(yt * 16, 16), 16)], rby.at[d], yb_ss.at[0], yb_rs.at[0], dev(x, yt, z, c)
        )
        cp.start()
    part = rgr.at[pl.ds(0, 15)]
    remote(part, part, g_ss.at[0], g_rs.at[0], sib).wait_recv()
    for g in range(NX):
        acc = rgr[g * 4].astype(F32)
        for i in range(1, 4):
            acc += rgr[g * 4 + i].astype(F32)
        acc = acc.astype(BF)
        o_rdk[0, :, g * HD : (g + 1) * HD] = acc[0:16, :]
        o_rdv[0, :, g * HD : (g + 1) * HD] = acc[16:32, :]

    some = rbz.at[pl.ds(1, 7)]
    remote(some, some, zb_ss.at[0], zb_rs.at[0], sib).wait_recv()
    acc = bdy[pl.ds(pl.multiple_of(z * 16, 16), 16), :].astype(F32)
    for d in range(1, 8):
        acc += rbz[d].astype(F32)
    fin[0:16, :] = acc.astype(BF)
    remote(some, some, yb_ss.at[0], yb_rs.at[0], sib).wait_recv()
    acc = bdz[pl.ds(pl.multiple_of(y * 16, 16), 16), :].astype(F32)
    for d in range(1, 8):
        acc += rby[d].astype(F32)
    fin[16:32, :] = acc.astype(BF)

    xo = 2 * zl + c
    zf, cf = x // 2, x % 2

    def final(i):
        zz, cc = i // 2, i % 2
        same = (xo == x) & (zl == zz) & (c == cc)
        return same, remote(fin, rfin.at[x], f_ss.at[i], f_rs.at[x], dev(xo, y, zh * 2 + zz, cc))

    for i in range(4):
        same, cp = final(i)

        @pl.when(jnp.logical_not(same))
        def _():
            cp.start()

        @pl.when(same)
        def _():
            rfin[x] = fin[...]

    for xs in range(NX):
        mine = (x == xs) & (zf == zl) & (cf == c)

        @pl.when(jnp.logical_not(mine))
        def _():
            remote(fin, rfin.at[xs], f_ss.at[0], f_rs.at[xs], sib).wait_recv()

    spot = zl * 2 + c
    for xs in range(NX):
        tile = rfin[xs].astype(F32)
        for half, out in ((0, o_dk), (16, o_dv)):
            rows = tile[half : half + 4, :]
            for i in range(1, 4):
                rows = jnp.where(spot == i, tile[half + 4 * i : half + 4 * i + 4, :], rows)
            out[:, xs * HD : (xs + 1) * HD] = rows.astype(BF)

    for i in range(4):
        same, cp = final(i)

        @pl.when(jnp.logical_not(same))
        def _():
            cp.wait_send()

    def sent(part, sem):
        remote(part, part, sem.at[0], p_rs.at[0, 0], sib).wait_send()

    sent(gout.at[0, pl.ds(0, 3), pl.ds(0, 384)], p_ss)
    sent(rtab.at[pl.ds(0, 15)], q_ss)
    sent(gout.at[0, pl.ds(0, 2), pl.ds(0, 384)], h_ss)
    sent(table.at[0], d_ss)
    sent(gout.at[0], e_ss)
    sent(seven, ya_ss)
    sent(seven, za_ss)
    sent(some, yb_ss)
    sent(some, zb_ss)
    sent(rtab.at[pl.ds(0, 15)], g_ss)
    pltpu.make_async_copy(dqs, dqs, in_sem.at[7]).wait()


def place(*refs):
    for i in range(6):
        refs[6 + i][...] = refs[i][...]


def shards(*args):
    hbm = pl.BlockSpec(memory_space=pl.ANY)
    vmem = pl.BlockSpec(memory_space=pltpu.VMEM)
    dma = pltpu.SemaphoreType.DMA
    shape = jax.ShapeDtypeStruct
    made = pl.pallas_call(
        kernel,
        out_shape=(
            shape((PROWS, 256), BF),
            shape((4, 512), BF),
            shape((4, 512), BF),
            shape((1, RESP, 256), BF),
            shape((1, 16, 512), BF),
            shape((1, 16, 512), BF),
        ),
        in_specs=[hbm] * 13,
        out_specs=(hbm, vmem, vmem, hbm, vmem, vmem),
        scratch_shapes=[
            pltpu.VMEM((LANES, HD), BF),
            pltpu.VMEM((LANES, HD), BF),
            pltpu.VMEM((LANES, HD), BF),
            pltpu.VMEM((128, 512), BF),
            pltpu.VMEM((4, 128, HD), BF),
            pltpu.VMEM((2, 4, 2, GROUP // 2, HD), BF),
            pltpu.VMEM((4, 32, HD), BF),
            pltpu.VMEM((16, 32, HD), BF),
            pltpu.VMEM((RESP, HD), BF),
            pltpu.VMEM((RESP, HD), BF),
            pltpu.VMEM((4, GROUP, LANES), F32),
            pltpu.VMEM((RESP, RL), F32),
            pltpu.VMEM((LANES, HD), BF),
            pltpu.VMEM((HD, LANES), F32),
            pltpu.VMEM((4, 1, LANES), F32),
            pltpu.VMEM((4, 1, LANES), F32),
            pltpu.VMEM((2, 4, GROUP, HD), BF),
            pltpu.VMEM((2, 4, 256, HD), BF),
            pltpu.VMEM((8, 128, HD), BF),
            pltpu.VMEM((8, 128, HD), BF),
            pltpu.VMEM((8, 128, HD), BF),
            pltpu.VMEM((8, 128, HD), BF),
            pltpu.VMEM((128, HD), BF),
            pltpu.VMEM((128, HD), BF),
            pltpu.VMEM((8, 16, HD), BF),
            pltpu.VMEM((8, 16, HD), BF),
            pltpu.VMEM((32, HD), BF),
            pltpu.VMEM((4, 32, HD), BF),
            pltpu.VMEM((16, 32, HD), BF),
            pltpu.VMEM((16, 32, HD), BF),
            pltpu.SMEM((4, 4), F32),
            pltpu.SMEM((1,), jnp.int32),
            dma((8,)),
            dma((1,)),
            dma((5, 2)),
            dma((1,)),
            dma((1,)),
            dma((1,)),
            dma((4, 2)),
            dma((1,)),
            dma((4,)),
            dma((1,)),
            dma((4,)),
        ]
        + [dma((1,))] * 8
        + [dma((4,)), dma((4,)), dma((1,)), dma((1,))],
        compiler_params=pltpu.CompilerParams(
            collective_id=0, has_side_effects=True, vmem_limit_bytes=60 * 1024 * 1024
        ),
        name="attention_backward",
    )(*args)
    return pl.pallas_call(
        place,
        out_shape=tuple(shape(a.shape, a.dtype) for a in made),
        in_specs=[vmem] * 6,
        out_specs=[vmem] * 6,
        compiler_params=pltpu.CompilerParams(vmem_limit_bytes=60 * 1024 * 1024),
        name="place_outputs",
    )(*made)


def solution(mesh):
    wide = P("sample", "prompt")
    block = P("prompt", None)
    resp = P("sample", None, "prompt")
    near = P("sample", "prompt", None)
    owned = P(("prompt", "sample"), None)
    return jax.shard_map(
        shards,
        mesh=mesh,
        in_specs=(wide, wide, wide, block, block, block, block, resp, resp, resp, near, near, P("sample")),
        out_specs=(wide, owned, owned, resp, near, near),
        check_vma=False,
    )
```

time: 63.6 us -> 58.2 us (0.915)
  Pallas kernels: 62.1 us -> 56.8 us
    pallas_call x1, Pallas kernels: 60.5 us -> 55.2 us  [shards(): pl.pallas_call(kernel, out_shape=(shape((PROWS, 256), BF), shape((4, 512)...]
where the time goes in v3:
time: 58.2 us; the launch traced here: 58.1 us
  Pallas kernels  56.8 us (98%)
  between operations  1.29 us (2%)
    pallas_call x1, Pallas kernels, shards(): pl.pallas_call(kernel, out_shape=(shape((PROWS, 256), BF), shape((4, 512)...  55.2 us
    pallas_call x1, Pallas kernels, shards(): pl.pallas_call(place, out_shape=tuple((shape(a.shape, a.dtype) for a in m...  1.6 us

profile of v3, /device:TPU:1, one launch (start us, length us, event | category | flops | bytes accessed | tf_op | source)
XLA Modules:
  0.0 58.1 jit_solution(12506761561379995497)
XLA Ops:
  1.3 55.2 %attention_backward.1 = (bf16[64,256]{1,0:T(8,128)(2,1)}, bf16[4,512]{1,0:T(4,128)(2,1)}, bf16[4,512]{1,0:T(4,128)(2,1)}, bf16[1,256,256]{2,1,0:T(8,128)(2,1)}, ...) custom-call(bf16[64,256]{1,0:T(8,128)(2,1)} %pq.1, bf16[64,256]{1,0:T(8,128)(2,1)} %pg.1, bf16[64,256]{1,0:T(8,128)(2,1)} %po.1, ...), custom_call_target="tpu_custom_call" | custom-call | tf_op jit(solution)/shard_map/attention_backward/pallas_call | solution.py:470
  56.5 1.6 %place_outputs.1 = (bf16[64,256]{1,0:T(8,128)(2,1)}, bf16[4,512]{1,0:T(4,128)(2,1)}, bf16[4,512]{1,0:T(4,128)(2,1)}, bf16[1,256,256]{2,1,0:T(8,128)(2,1)}, bf16[...) custom-call(bf16[64,256]{1,0:T(8,128)(2,1)} %get-tuple-element.12.refs_0_, bf16[4,512]{1,0:T(4,128)(2,1)} %get-tuple-element.13.refs_1_, ...), custom_call_target="tpu_custom_call" | custom-call | tf_op jit(solution)/shard_map/place_outputs/pallas_call | solution.py:534

commit v4 on v3

--- a/solution.py
+++ b/solution.py
@@ -39,7 +39,7 @@
 def kernel(
     pq, pg, po, kc, vc, ks, vs, rq, rg, ro, rk, rv, ln,
     o_dq, o_dk, o_dv, o_rdq, o_rdk, o_rdv,
-    qm, gm, om, codes, deq, table, rsend, rtab, kr, vr, S, Sr, dqs, dqt,
+    qm, gm, om, codes, deq, table, rsend, rtab, kr, vr, S, DP, Sr, dqs, dqt,
     mx, sm, gout, r1, ady, adz, ray, raz, bdy, bdz, rby, rbz, fin, rfin, rgs, rgr, scl, lens,
     in_sem,
     p_ss, p_rs, q_ss, q_rs, h_ss, h_rs, d_ss, d_rs, e_ss, e_rs, ya_ss, ya_rs, za_ss, za_rs,
@@ -135,15 +135,15 @@
         src = deq.at[xt, pl.ds(pl.multiple_of(half * HALF, HALF), HALF)]
         remote(src, table.at[c, zh, half, own_rows], p_ss.at[0], sem, dev(xt, y, zt, c)).start()
 
-    for d in (1, 2, 3):
-        for dx in (2, 1, 3, 0):
-            psend(wrap(x + dx, NX), wrap(z + sg * d, NZ), hy, p_rs.at[zh, x // 2])
+    for dx in (2, 1, 3, 0):
+        psend(wrap(x + dx, NX), wrap(z + 1 * sg, NZ), hy, p_rs.at[zh, x // 2])
+    for dx in (2, 1, 3, 0):
+        psend(wrap(x + dx, NX), wrap(z + 2 * sg, NZ), hy, p_rs.at[zh, x // 2])
+    for dx in (2, 1, 3, 0):
+        psend(wrap(x + dx, NX), wrap(z + 3 * sg, NZ), hy, p_rs.at[zh, x // 2])
     for dx in (2, 1, 3):
         for half in range(2):
             psend(wrap(x + dx, NX), z, half, p_rs.at[4, 0])
-    for k in range(1, 16):
-        pt = wrap(p + k, 16)
-        remote(rsend.at[pt // 4], rtab.at[p], q_ss.at[0], q_rs.at[0], (pt, s)).start()
     rtab[p] = rsend[x]
 
     groups = [zh, wrap(zh + sg, NZH), wrap(zh - sg, NZH), wrap(zh + 2, NZH)]
@@ -173,6 +173,11 @@
             remote(part, part, p_ss.at[0], p_rs.at[zg, i], sib).wait_recv()
             remote(part, part, h_ss.at[0], h_rs.at[zg, i], dev(x, wrap(y + 1 - 2 * i, NY), z, c)).start()
         hand(k, table.at[c, zg, hy])
+
+    def take_whole(k):
+        part = table.at[c, groups[k]]
+        remote(part, part, p_ss.at[0], p_rs.at[groups[k], 0], sib).wait_recv()
+        hand(k, part)
 
     def take_beside(k):
         zg = groups[k]
@@ -206,22 +211,24 @@
         own = jnp.exp2((own - best) * (inv * LOG2E))
         sm[zg, :, RL:LANES] = jnp.sum(own, axis=0, keepdims=True)
         S[zg, :, RL:LANES] = own
+        DP[zg] = dot_t(table[1, zg].reshape(GROUP, HD), gm[...]) - delta
+
+    def absorb_loop(k, _):
+        absorb(k)
+        return 0
 
     take_near()
     take_far(1)
     absorb(0)
     take_far(2)
     take_far(3)
+    for k in range(1, 16):
+        pt = wrap(p + k, 16)
+        remote(rsend.at[pt // 4], rtab.at[p], q_ss.at[0], q_rs.at[0], (pt, s)).start()
     take_beside(1)
     take_beside(2)
     take_beside(3)
-
-    def absorb_loop(k, _):
-        absorb(k)
-        return 0
-
     lax.fori_loop(1, 4, absorb_loop, 0)
-
     part = rtab.at[pl.ds(0, 15)]
     remote(part, part, q_ss.at[0], q_rs.at[0], sib).wait_recv()
     for i in range(16):
@@ -242,6 +249,7 @@
     tops = jnp.concatenate(tops + [jnp.full((1, 2 * PROWS), NEG, F32)], axis=1)
     sums = jnp.concatenate(sums + [jnp.zeros((1, 2 * PROWS), F32)], axis=1)
 
+
     top = tops
     for zg in range(4):
         top = jnp.maximum(top, mx[zg])
@@ -256,6 +264,21 @@
     rscale = rscale * rtotal
     for zg in range(4):
         mx[zg] = scales[zg] * rtotal
+
+    prob = Sr[...] * rscale[:, 0:RL]
+    dp = dot_t(vr[...], gm[0:RL, :])
+    ds = (prob * (dp - delta[:, 0:RL])).astype(BF)
+    dqt[:, 0:RL] = dot_l(kr[...], ds)
+    dqt[:, RL:LANES] = jnp.zeros((HD, 2 * PROWS), F32)
+    dkr = (dot_n(ds, qm[0:RL, :]) * inv).astype(BF)
+    dvr = dot_n(prob.astype(BF), gm[0:RL, :]).astype(BF)
+    for i in range(16):
+        rgs[i, 0:16, :] = dkr[i * 16 : (i + 1) * 16, :]
+        rgs[i, 16:32, :] = dvr[i * 16 : (i + 1) * 16, :]
+    for k in range(1, 16):
+        pt = wrap(p + k, 16)
+        remote(rgs.at[pt], rgr.at[p], g_ss.at[0], g_rs.at[0], (pt, s)).start()
+    rgr[p] = rgs[p]
 
     def pair(zg, kv, i):
         rows = pl.ds(pl.multiple_of((2 * i + 1 - c) * 128, 128), 128)
@@ -297,8 +320,7 @@
     def grads(k, _):
         zg = group_of(k)
         prob = S[zg] * mx[zg]
-        dp = dot_t(table[1, zg].reshape(GROUP, HD), gm[...])
-        ds = (prob * (dp - delta)).astype(BF)
+        ds = (prob * DP[zg]).astype(BF)
         dqt[...] += dot_l(table[0, zg].reshape(GROUP, HD), ds)
         for kv in range(2):
             if kv == 0:
@@ -314,29 +336,13 @@
             for i in range(2):
                 pair(zg, kv, i).start()
 
-        @pl.when(k > 0)
-        def _():
+        if k > 0:
             spread(k - 1)
 
         return 0
 
-    dqt[...] = jnp.zeros_like(dqt)
-    lax.fori_loop(0, 4, grads, 0)
-
-    prob = Sr[...] * rscale[:, 0:RL]
-    dp = dot_t(vr[...], gm[0:RL, :])
-    ds = (prob * (dp - delta[:, 0:RL])).astype(BF)
-    dqt[:, 0:RL] += dot_l(kr[...], ds)
-    dkr = (dot_n(ds, qm[0:RL, :]) * inv).astype(BF)
-    dvr = dot_n(prob.astype(BF), gm[0:RL, :]).astype(BF)
-    for i in range(16):
-        rgs[i, 0:16, :] = dkr[i * 16 : (i + 1) * 16, :]
-        rgs[i, 16:32, :] = dvr[i * 16 : (i + 1) * 16, :]
-    spread(3)
-    for k in range(1, 16):
-        pt = wrap(p + k, 16)
-        remote(rgs.at[pt], rgr.at[p], g_ss.at[0], g_rs.at[0], (pt, s)).start()
-    rgr[p] = rgs[p]
+    for k in range(4):
+        grads(k, 0)
 
     dqs[...] = (dqt[...].T * inv).astype(BF)
     outs = []
@@ -354,6 +360,7 @@
     for cp in outs:
         cp.start()
 
+    spread(3)
     seven = ray.at[pl.ds(1, 7)]
     remote(seven, seven, ya_ss.at[0], ya_rs.at[0], sib).wait_recv()
     acc = ady[y].astype(F32)
@@ -377,16 +384,6 @@
             bdz.at[pl.ds(pl.multiple_of(yt * 16, 16), 16)], rby.at[d], yb_ss.at[0], yb_rs.at[0], dev(x, yt, z, c)
         )
         cp.start()
-    part = rgr.at[pl.ds(0, 15)]
-    remote(part, part, g_ss.at[0], g_rs.at[0], sib).wait_recv()
-    for g in range(NX):
-        acc = rgr[g * 4].astype(F32)
-        for i in range(1, 4):
-            acc += rgr[g * 4 + i].astype(F32)
-        acc = acc.astype(BF)
-        o_rdk[0, :, g * HD : (g + 1) * HD] = acc[0:16, :]
-        o_rdv[0, :, g * HD : (g + 1) * HD] = acc[16:32, :]
-
     some = rbz.at[pl.ds(1, 7)]
     remote(some, some, zb_ss.at[0], zb_rs.at[0], sib).wait_recv()
     acc = bdy[pl.ds(pl.multiple_of(z * 16, 16), 16), :].astype(F32)
@@ -418,6 +415,16 @@
         def _():
             rfin[x] = fin[...]
 
+    part = rgr.at[pl.ds(0, 15)]
+    remote(part, part, g_ss.at[0], g_rs.at[0], sib).wait_recv()
+    for g in range(NX):
+        acc = rgr[g * 4].astype(F32)
+        for i in range(1, 4):
+            acc += rgr[g * 4 + i].astype(F32)
+        acc = acc.astype(BF)
+        o_rdk[0, :, g * HD : (g + 1) * HD] = acc[0:16, :]
+        o_rdv[0, :, g * HD : (g + 1) * HD] = acc[16:32, :]
+
     for xs in range(NX):
         mine = (x == xs) & (zf == zl) & (cf == c)
 
@@ -446,7 +453,7 @@
 
     sent(gout.at[0, pl.ds(0, 3), pl.ds(0, 384)], p_ss)
     sent(rtab.at[pl.ds(0, 15)], q_ss)
-    sent(gout.at[0, pl.ds(0, 2), pl.ds(0, 384)], h_ss)
+    sent(gout.at[0, pl.ds(0, 3), pl.ds(0, 256)], h_ss)
     sent(table.at[0], d_ss)
     sent(gout.at[0], e_ss)
     sent(seven, ya_ss)
@@ -490,6 +497,7 @@
             pltpu.VMEM((16, 32, HD), BF),
             pltpu.VMEM((RESP, HD), BF),
             pltpu.VMEM((RESP, HD), BF),
+            pltpu.VMEM((4, GROUP, LANES), F32),
             pltpu.VMEM((4, GROUP, LANES), F32),
             pltpu.VMEM((RESP, RL), F32),
             pltpu.VMEM((LANES, HD), BF),

time: 58.2 us -> 56.5 us (0.971)
  Pallas kernels: 56.8 us -> 55.1 us
    pallas_call x1, Pallas kernels: 55.2 us -> 53.5 us  [shards(): pl.pallas_call(kernel, out_shape=(shape((PROWS, 256), BF), shape((4, 512)...]
where the time goes in v4:
time: 56.5 us; the launch traced here: 56.4 us
  Pallas kernels  55.1 us (98%)
  between operations  1.29 us (2%)
    pallas_call x1, Pallas kernels, shards(): pl.pallas_call(kernel, out_shape=(shape((PROWS, 256), BF), shape((4, 512)...  53.5 us
    pallas_call x1, Pallas kernels, shards(): pl.pallas_call(place, out_shape=tuple((shape(a.shape, a.dtype) for a in m...  1.6 us

profile of v4, /device:TPU:1, one launch (start us, length us, event | category | flops | bytes accessed | tf_op | source)
XLA Modules:
  0.0 56.4 jit_solution(3294420413519345667)
XLA Ops:
  1.3 53.5 %attention_backward.1 = (bf16[64,256]{1,0:T(8,128)(2,1)}, bf16[4,512]{1,0:T(4,128)(2,1)}, bf16[4,512]{1,0:T(4,128)(2,1)}, bf16[1,256,256]{2,1,0:T(8,128)(2,1)}, ...) custom-call(bf16[64,256]{1,0:T(8,128)(2,1)} %pq.1, bf16[64,256]{1,0:T(8,128)(2,1)} %pg.1, bf16[64,256]{1,0:T(8,128)(2,1)} %po.1, ...), custom_call_target="tpu_custom_call" | custom-call | tf_op jit(solution)/shard_map/attention_backward/pallas_call | solution.py:477
  54.8 1.6 %place_outputs.1 = (bf16[64,256]{1,0:T(8,128)(2,1)}, bf16[4,512]{1,0:T(4,128)(2,1)}, bf16[4,512]{1,0:T(4,128)(2,1)}, bf16[1,256,256]{2,1,0:T(8,128)(2,1)}, bf16[...) custom-call(bf16[64,256]{1,0:T(8,128)(2,1)} %get-tuple-element.12.refs_0_, bf16[4,512]{1,0:T(4,128)(2,1)} %get-tuple-element.13.refs_1_, ...), custom_call_target="tpu_custom_call" | custom-call | tf_op jit(solution)/shard_map/place_outputs/pallas_call | solution.py:542

commit v5 on v4

--- a/solution.py
+++ b/solution.py
@@ -39,7 +39,7 @@
 def kernel(
     pq, pg, po, kc, vc, ks, vs, rq, rg, ro, rk, rv, ln,
     o_dq, o_dk, o_dv, o_rdq, o_rdk, o_rdv,
-    qm, gm, om, codes, deq, table, rsend, rtab, kr, vr, S, DP, Sr, dqs, dqt,
+    qm, gm, om, codes, deq, table, rsend, rtab, kr, vr, S, DP, Sr, dqt,
     mx, sm, gout, r1, ady, adz, ray, raz, bdy, bdz, rby, rbz, fin, rfin, rgs, rgr, scl, lens,
     in_sem,
     p_ss, p_rs, q_ss, q_rs, h_ss, h_rs, d_ss, d_rs, e_ss, e_rs, ya_ss, ya_rs, za_ss, za_rs,
@@ -344,21 +344,10 @@
     for k in range(4):
         grads(k, 0)
 
-    dqs[...] = (dqt[...].T * inv).astype(BF)
-    outs = []
+    dqs = (dqt[...].T * inv).astype(BF)
     for h in range(2):
-        outs.append(
-            pltpu.make_async_copy(
-                dqs.at[pl.ds(h * RESP, RESP)], o_rdq.at[0, :, pl.ds(h * HD, HD)], in_sem.at[7]
-            )
-        )
-        outs.append(
-            pltpu.make_async_copy(
-                dqs.at[pl.ds(RL + h * PROWS, PROWS)], o_dq.at[:, pl.ds(h * HD, HD)], in_sem.at[7]
-            )
-        )
-    for cp in outs:
-        cp.start()
+        o_rdq[0, :, h * HD : (h + 1) * HD] = dqs[h * RESP : (h + 1) * RESP, :]
+        o_dq[:, h * HD : (h + 1) * HD] = dqs[RL + h * PROWS : RL + (h + 1) * PROWS, :]
 
     spread(3)
     seven = ray.at[pl.ds(1, 7)]
@@ -461,7 +450,6 @@
     sent(some, yb_ss)
     sent(some, zb_ss)
     sent(rtab.at[pl.ds(0, 15)], g_ss)
-    pltpu.make_async_copy(dqs, dqs, in_sem.at[7]).wait()
 
 
 def place(*refs):
@@ -470,22 +458,22 @@
 
 
 def shards(*args):
-    hbm = pl.BlockSpec(memory_space=pl.ANY)
+    hbm = pl.BlockSpec(memory_space=pltpu.HBM)
     vmem = pl.BlockSpec(memory_space=pltpu.VMEM)
     dma = pltpu.SemaphoreType.DMA
     shape = jax.ShapeDtypeStruct
     made = pl.pallas_call(
         kernel,
         out_shape=(
-            shape((PROWS, 256), BF),
-            shape((4, 512), BF),
-            shape((4, 512), BF),
-            shape((1, RESP, 256), BF),
-            shape((1, 16, 512), BF),
-            shape((1, 16, 512), BF),
+            pltpu.VMEM((PROWS, 256), BF),
+            pltpu.VMEM((4, 512), BF),
+            pltpu.VMEM((4, 512), BF),
+            pltpu.VMEM((1, RESP, 256), BF),
+            pltpu.VMEM((1, 16, 512), BF),
+            pltpu.VMEM((1, 16, 512), BF),
         ),
         in_specs=[hbm] * 13,
-        out_specs=(hbm, vmem, vmem, hbm, vmem, vmem),
+        out_specs=[vmem] * 6,
         scratch_shapes=[
             pltpu.VMEM((LANES, HD), BF),
             pltpu.VMEM((LANES, HD), BF),
@@ -500,7 +488,6 @@
             pltpu.VMEM((4, GROUP, LANES), F32),
             pltpu.VMEM((4, GROUP, LANES), F32),
             pltpu.VMEM((RESP, RL), F32),
-            pltpu.VMEM((LANES, HD), BF),
             pltpu.VMEM((HD, LANES), F32),
             pltpu.VMEM((4, 1, LANES), F32),
             pltpu.VMEM((4, 1, LANES), F32),
@@ -520,7 +507,7 @@
             pltpu.VMEM((16, 32, HD), BF),
             pltpu.SMEM((4, 4), F32),
             pltpu.SMEM((1,), jnp.int32),
-            dma((8,)),
+            dma((7,)),
             dma((1,)),
             dma((5, 2)),
             dma((1,)),
@@ -535,16 +522,16 @@
         + [dma((1,))] * 8
         + [dma((4,)), dma((4,)), dma((1,)), dma((1,))],
         compiler_params=pltpu.CompilerParams(
-            collective_id=0, has_side_effects=True, vmem_limit_bytes=60 * 1024 * 1024
+            collective_id=0, has_side_effects=True, vmem_limit_bytes=61440 * 1024
         ),
         name="attention_backward",
     )(*args)
     return pl.pallas_call(
         place,
-        out_shape=tuple(shape(a.shape, a.dtype) for a in made),
+        out_shape=tuple(shape(a.shape, BF) for a in made),
         in_specs=[vmem] * 6,
         out_specs=[vmem] * 6,
-        compiler_params=pltpu.CompilerParams(vmem_limit_bytes=60 * 1024 * 1024),
+        compiler_params=pltpu.CompilerParams(vmem_limit_bytes=40 * 1024 * 1024),
         name="place_outputs",
     )(*made)
 

time: 56.5 us -> 55 us (0.973)
  Pallas kernels: 55.1 us -> 53.5 us
    pallas_call x2, Pallas kernels: 55.1 us -> 53.5 us  [the longest x1 52.8 us: shards(): pl.pallas_call(kernel, out_shape=(pltpu.VMEM((PROWS, 256), BF), pltpu.VME...]
where the time goes in v5:
time: 55 us; the launch traced here: 54.8 us
  Pallas kernels  53.5 us (97%)
  between operations  1.29 us (2%)
    pallas_call x1, Pallas kernels, shards(): pl.pallas_call(kernel, out_shape=(pltpu.VMEM((PROWS, 256), BF), pltpu.VME...  52.8 us

profile of v5, /device:TPU:1, one launch (start us, length us, event | category | flops | bytes accessed | tf_op | source)
XLA Modules:
  0.0 54.8 jit_solution(9885722062614334021)
XLA Ops:
  1.3 52.8 %attention_backward.1 = (bf16[64,256]{1,0:T(8,128)(2,1)S(1)}, bf16[4,512]{1,0:T(4,128)(2,1)S(1)}, bf16[4,512]{1,0:T(4,128)(2,1)S(1)}, bf16[1,256,256]{2,1,0:T(8,...) custom-call(bf16[64,256]{1,0:T(8,128)(2,1)} %pq.1, bf16[64,256]{1,0:T(8,128)(2,1)} %pg.1, ...), custom_call_target="tpu_custom_call" | custom-call | tf_op jit(solution)/shard_map/attention_backward/pallas_call | solution.py:465
  54.1 0.7 %place_outputs.1 = (bf16[64,256]{1,0:T(8,128)(2,1)}, bf16[4,512]{1,0:T(4,128)(2,1)}, bf16[4,512]{1,0:T(4,128)(2,1)}, bf16[1,256,256]{2,1,0:T(8,128)(2,1)}, bf16[...) custom-call(bf16[64,256]{1,0:T(8,128)(2,1)S(1)} %get-tuple-element.12.refs_0_, ...), custom_call_target="tpu_custom_call" | custom-call | tf_op jit(solution)/shard_map/place_outputs/pallas_call | solution.py:529

commit v6 on v5

--- a/solution.py
+++ b/solution.py
@@ -68,9 +68,8 @@
     bar = pltpu.get_barrier_semaphore()
     partners = []
     for dx in range(NX):
-        for dz in range(NZ):
-            if dx or dz:
-                partners.append(dev(wrap(x + dx, NX), y, wrap(z + dz, NZ), c))
+        for dz in (0, 1, 2, 3, 4, 6) if dx else range(1, NZ):
+            partners.append(dev(wrap(x + dx, NX), y, wrap(z + sg * dz, NZ), c))
     for dy in range(1, NY):
         partners.append(dev(x, wrap(y + dy, NY), z, c))
     for dx in range(NX):

time: 55 us -> 54.9 us (level)
  no operation moved by 1% of the time
where the time goes in v6:
time: 54.9 us; the launch traced here: 54.8 us
  Pallas kernels  53.5 us (97%)
  between operations  1.29 us (2%)
    pallas_call x1, Pallas kernels, shards(): pl.pallas_call(kernel, out_shape=(pltpu.VMEM((PROWS, 256), BF), pltpu.VME...  52.8 us

profile of v6, /device:TPU:1, one launch (start us, length us, event | category | flops | bytes accessed | tf_op | source)
XLA Modules:
  0.0 54.8 jit_solution(1648655322751436923)
XLA Ops:
  1.3 52.8 %attention_backward.1 = (bf16[64,256]{1,0:T(8,128)(2,1)S(1)}, bf16[4,512]{1,0:T(4,128)(2,1)S(1)}, bf16[4,512]{1,0:T(4,128)(2,1)S(1)}, bf16[1,256,256]{2,1,0:T(8,...) custom-call(bf16[64,256]{1,0:T(8,128)(2,1)} %pq.1, bf16[64,256]{1,0:T(8,128)(2,1)} %pg.1, ...), custom_call_target="tpu_custom_call" | custom-call | tf_op jit(solution)/shard_map/attention_backward/pallas_call | solution.py:464
  54.1 0.7 %place_outputs.1 = (bf16[64,256]{1,0:T(8,128)(2,1)}, bf16[4,512]{1,0:T(4,128)(2,1)}, bf16[4,512]{1,0:T(4,128)(2,1)}, bf16[1,256,256]{2,1,0:T(8,128)(2,1)}, bf16[...) custom-call(bf16[64,256]{1,0:T(8,128)(2,1)S(1)} %get-tuple-element.12.refs_0_, ...), custom_call_target="tpu_custom_call" | custom-call | tf_op jit(solution)/shard_map/place_outputs/pallas_call | solution.py:528
